TPU v7x, 32 devices: a whole 2x2x4 slice. The times are simulated.
32 devices in a mesh: section: 2 (over core), seq: 8 (over z, y), mp: 2 (over x).
Axes of the slice: x: 2, y: 2, z: 4, core: 2. Of those that a mesh axis runs over, the one named last changes fastest.
Arguments:
- x_in: bfloat16 [2, 512, 8192], P(None, 'mp', 'seq'), may hold values from -14 to 14
- skip_in: float32 [2, 512, 8192], P(None, 'mp', 'seq'), may hold values from -6 to 6
- cot_res: float32 [2, 512, 8192], P(None, 'mp', 'seq'), may hold values from -6 to 6
- cot_skip: float32 [2, 512, 8192], P(None, 'mp', 'seq'), may hold values from -6 to 6
- lengths: int32 [2], replicated, may hold values from 4096 to 8192, as said below
- speakers: int32 [2], replicated, may hold values from 0 to 108
- conv_weight: float32 [2, 2, 512, 2, 512], P('section', None, None, None, 'mp'), may hold values from -0.1875 to 0.1875
- conv_m: float32 [2, 2, 512, 2, 512], P('section', None, None, None, 'mp'), may hold values from -80 to 80
- conv_v: float32 [2, 2, 512, 2, 512], P('section', None, None, None, 'mp'), may hold values from 13.1072 to 52.4288
- out_weight: float32 [2, 512, 1024], P('section', 'mp'), may hold values from -0.75 to 0.75
- out_m: float32 [2, 512, 1024], P('section', 'mp'), may hold values from -24 to 24
- out_v: float32 [2, 512, 1024], P('section', 'mp'), may hold values from 0.98304 to 4.096
- speaker_table: float32 [2, 109, 2, 512], P('section', None, None, 'mp'), may hold values from -3 to 3
- table_m: float32 [2, 109, 2, 512], P('section', None, None, 'mp'), may hold values from -56 to 56
- table_v: float32 [2, 109, 2, 512], P('section', None, None, 'mp'), may hold values from 6.5536 to 26.2144
Outputs:
- res_out: float32 [2, 2, 512, 8192], P('section', None, 'mp', 'seq')
- skip_out: float32 [2, 2, 512, 8192], P('section', None, 'mp', 'seq')
- grad_in: float32 [2, 2, 512, 8192], P('section', None, 'mp', 'seq')
- rms_out: float32 [2, 2], P('section')
- conv_grad: float32 [2, 2, 512, 2, 512], P('section', None, None, None, 'mp')
- conv_new: float32 [2, 2, 512, 2, 512], P('section', None, None, None, 'mp')
- conv_m_new: float32 [2, 2, 512, 2, 512], P('section', None, None, None, 'mp')
- conv_v_new: float32 [2, 2, 512, 2, 512], P('section', None, None, None, 'mp')
- out_grad: float32 [2, 512, 1024], P('section', 'mp')
- out_new: float32 [2, 512, 1024], P('section', 'mp')
- out_m_new: float32 [2, 512, 1024], P('section', 'mp')
- out_v_new: float32 [2, 512, 1024], P('section', 'mp')
- table_grad: float32 [2, 109, 2, 512], P('section', None, None, 'mp')
- table_new: float32 [2, 109, 2, 512], P('section', None, None, 'mp')
- table_m_new: float32 [2, 109, 2, 512], P('section', None, None, 'mp')
- table_v_new: float32 [2, 109, 2, 512], P('section', None, None, 'mp')
Inputs may be any that keep to these rules, and one draw needn't show every extreme that they name: lengths[m] counts the valid samples at the start of micro-batch m, after which its tail is masked; some micro-batch is valid over all 8192 samples.
All inputs are finite; a program needn't handle non-finite values.
Results may differ from a plain program's by a relative error of at most 0.0091.
Values may be sent and summed in bfloat16 or wider, within the bound.
A program may use at most 128 MiB of HBM per device.

v0:
```python
import math

import jax
import jax.numpy as jnp
from jax import lax
from jax.sharding import PartitionSpec as P

FIRST_DILATION = 512
STEP = 10


beta_one = 0.9
beta_two = 0.999
adam_eps = 1e-08
decay_rate = 0.01
root_half = math.sqrt(0.5)


def passed_along(value, axis, steps):
    count = lax.axis_size(axis)
    first, last = (max(0, -steps), min(count, count - steps))
    return lax.ppermute(value, axis, [(source, source + steps) for source in range(first, last)])


def adamw(weight, moment, second, gradient, step_rate):
    moment_new = beta_one * moment + (1.0 - beta_one) * gradient
    second_new = beta_two * second + (1.0 - beta_two) * gradient * gradient
    corr_one = 1.0 - beta_one**STEP
    corr_two = 1.0 - beta_two**STEP
    update = moment_new / corr_one / (jnp.sqrt(second_new / corr_two) + adam_eps)
    weight_new = weight - step_rate * (update + decay_rate * weight)
    return (weight_new, moment_new, second_new)


def shards(
    x_in,
    skip_in,
    cot_res,
    cot_skip,
    lengths,
    speakers,
    conv_weight,
    conv_m,
    conv_v,
    out_weight,
    out_m,
    out_v,
    speaker_table,
    table_m,
    table_v,
):
    micro_count, residual_local, block_length_rows = x_in.shape
    leading_section = lax.axis_index("section") == 0
    seq_index = lax.axis_index("seq")
    dilation_factor = jnp.where(leading_section, FIRST_DILATION, 1).astype(jnp.int32)
    conv_low = conv_weight[0].astype(jnp.bfloat16)
    full_res = conv_low.shape[1]
    gate_dev = conv_low.shape[3]
    speaker_rows = speaker_table.shape[1]
    conv_matrix = conv_low.reshape(2 * full_res, 2 * gate_dev)
    output_low = out_weight[0].astype(jnp.bfloat16)
    table_low = speaker_table[0].astype(jnp.bfloat16).reshape(speaker_rows, 2 * gate_dev)
    positions = seq_index * block_length_rows + jnp.arange(block_length_rows)
    contract_first = (((0,), (0,)), ((), ()))
    contract_last = (((1,), (1,)), ((), ()))
    recv_resid = jnp.zeros((residual_local, block_length_rows), jnp.float32)
    recv_skip = jnp.zeros((residual_local, block_length_rows), jnp.float32)
    kept_list = []
    resid_list = []
    skip_list = []
    square_res = jnp.float32(0.0)
    square_branch = jnp.float32(0.0)
    counted = jnp.float32(0.0)
    for tick_num in range(micro_count + 1):
        index_zero = min(tick_num, micro_count - 1)
        index_one = max(tick_num - 1, 0)
        batch_idx = jnp.where(leading_section, index_zero, index_one)
        is_live = jnp.where(leading_section, tick_num < micro_count, tick_num >= 1).astype(
            jnp.float32
        )
        residual_stream = jnp.where(
            leading_section, x_in[index_zero].astype(jnp.float32), recv_resid
        )
        skip_accumulated = jnp.where(leading_section, skip_in[index_zero], recv_skip)
        onehot = (jnp.arange(speaker_rows) == speakers[batch_idx]).astype(jnp.bfloat16)
        input_signal = residual_stream.astype(jnp.bfloat16)
        preceding_state = passed_along(
            input_signal[:, block_length_rows - FIRST_DILATION :], "seq", 1
        )
        joined_taps = jnp.concatenate([preceding_state, input_signal], axis=1)
        delayed_tap = lax.dynamic_slice_in_dim(
            joined_taps, FIRST_DILATION - dilation_factor, block_length_rows, 1
        )
        tap_rows = jnp.stack([delayed_tap, input_signal], axis=0)
        forward_tap_full = lax.all_gather(tap_rows, "mp", axis=1, tiled=True).reshape(
            2 * full_res, block_length_rows
        )
        embedding = jnp.dot(onehot, table_low, preferred_element_type=jnp.float32)
        forward_preact = (
            lax.dot_general(
                conv_matrix, forward_tap_full, contract_first, preferred_element_type=jnp.float32
            )
            + embedding[:, None]
        )
        hidden = (
            jnp.tanh(forward_preact[:gate_dev]) * jax.nn.sigmoid(forward_preact[gate_dev:])
        ).astype(jnp.bfloat16)
        partial_sums = lax.dot_general(
            output_low, hidden, contract_first, preferred_element_type=jnp.float32
        ).reshape(2, full_res, block_length_rows)
        projected = lax.psum_scatter(partial_sums, "mp", scatter_dimension=1, tiled=True)
        branch = projected[0]
        new_resid = (residual_stream + branch) * root_half
        new_skip = skip_accumulated + projected[1]
        new_resid, new_skip, branch, kept_data = (
            new_resid,
            new_skip,
            branch,
            (forward_tap_full, forward_preact, hidden),
        )
        valid_rows = (positions < lengths[batch_idx]).astype(jnp.float32)[None, :] * is_live
        square_res = square_res + jnp.sum(valid_rows * new_resid * new_resid)
        square_branch = square_branch + jnp.sum(valid_rows * branch * branch)
        counted = counted + jnp.sum(valid_rows) * residual_local
        kept_list.append(kept_data)
        resid_list.append(new_resid)
        skip_list.append(new_skip)
        if tick_num < micro_count:
            recv_resid, recv_skip = passed_along((new_resid, new_skip), "section", 1)
    square_res, square_branch, counted = lax.psum(
        (square_res, square_branch, counted), ("seq", "mp")
    )
    rms_out = jnp.stack([jnp.sqrt(square_res / counted), jnp.sqrt(square_branch / counted)])[None]
    res_out = jnp.stack(
        [
            jnp.where(leading_section, resid_list[m_idx], resid_list[m_idx + 1])
            for m_idx in range(micro_count)
        ]
    )[None]
    skip_out = jnp.stack(
        [
            jnp.where(leading_section, skip_list[m_idx], skip_list[m_idx + 1])
            for m_idx in range(micro_count)
        ]
    )[None]
    conv_acc = jnp.zeros((2 * full_res, 2 * gate_dev), jnp.float32)
    table_acc = jnp.zeros((speaker_rows, 2 * gate_dev), jnp.float32)
    out_acc = jnp.zeros((gate_dev, 2 * full_res), jnp.float32)
    recv_grad = jnp.zeros((residual_local, block_length_rows), jnp.float32)
    input_grads = []
    for tick_num in range(micro_count + 1):
        index_one = min(tick_num, micro_count - 1)
        index_zero = max(tick_num - 1, 0)
        batch_idx = jnp.where(leading_section, index_zero, index_one)
        is_live = jnp.where(leading_section, tick_num >= 1, tick_num < micro_count).astype(
            jnp.float32
        )
        valid_rows = (positions < lengths[batch_idx]).astype(jnp.float32)[None, :] * is_live
        onehot = (jnp.arange(speaker_rows) == speakers[batch_idx]).astype(jnp.bfloat16)
        kept_data = jax.tree.map(
            lambda zero_side, one_side: jnp.where(leading_section, zero_side, one_side),
            kept_list[index_zero],
            kept_list[index_one + 1],
        )
        skip_grad = (
            jnp.where(leading_section, cot_skip[index_zero], cot_skip[index_one]) * valid_rows
        )
        resid_grad = jnp.where(
            leading_section, recv_grad * is_live, cot_res[index_one] * valid_rows
        )
        tap_full, preact, hidden_used = kept_data
        proj_grad = jnp.stack([resid_grad * root_half, skip_grad], axis=0).astype(jnp.bfloat16)
        full_grad = lax.all_gather(proj_grad, "mp", axis=1, tiled=True).reshape(
            2 * full_res, block_length_rows
        )
        hidden_grad = jnp.dot(output_low, full_grad, preferred_element_type=jnp.float32)
        weight_term = lax.dot_general(
            hidden_used, full_grad, contract_last, preferred_element_type=jnp.float32
        )
        filter_act = jnp.tanh(preact[:gate_dev])
        gate_act = jax.nn.sigmoid(preact[gate_dev:])
        filter_grad = hidden_grad * gate_act * (1.0 - filter_act * filter_act)
        gate_grad = hidden_grad * filter_act * gate_act * (1.0 - gate_act)
        preact_grad = jnp.concatenate([filter_grad, gate_grad], axis=0).astype(jnp.bfloat16)
        conv_term = lax.dot_general(
            tap_full, preact_grad, contract_last, preferred_element_type=jnp.float32
        )
        column_sums = jnp.sum(preact_grad.astype(jnp.float32), axis=1)
        table_term = onehot.astype(jnp.float32)[:, None] * column_sums[None, :]
        tap_terms = jnp.dot(conv_matrix, preact_grad, preferred_element_type=jnp.float32)
        tap_gradient = lax.psum_scatter(
            tap_terms.reshape(2, full_res, block_length_rows), "mp", scatter_dimension=1, tiled=True
        )
        joined_taps_gradient = lax.dynamic_update_slice_in_dim(
            jnp.zeros((residual_local, FIRST_DILATION + block_length_rows), jnp.float32),
            tap_gradient[0],
            FIRST_DILATION - dilation_factor,
            1,
        )
        border_gradient = passed_along(joined_taps_gradient[:, :FIRST_DILATION], "seq", -1)
        input_gradient_rows = tap_gradient[1] + joined_taps_gradient[:, FIRST_DILATION:]
        input_gradient_rows = input_gradient_rows.at[:, block_length_rows - FIRST_DILATION :].add(
            border_gradient
        )
        resid_back, conv_term, weight_term, table_term = (
            resid_grad * root_half + input_gradient_rows,
            conv_term,
            weight_term,
            table_term,
        )
        conv_acc = conv_acc + conv_term
        out_acc = out_acc + weight_term
        table_acc = table_acc + table_term
        input_grads.append(resid_back)
        if tick_num < micro_count:
            recv_grad = passed_along(resid_back, "section", -1)
    grad_in = jnp.stack(
        [
            jnp.where(leading_section, input_grads[m_idx + 1], input_grads[m_idx])
            for m_idx in range(micro_count)
        ]
    )[None]
    conv_total, out_total, table_total = lax.psum((conv_acc, out_acc, table_acc), "seq")
    conv_grad = conv_total.reshape(conv_weight.shape)
    out_grad = out_total.reshape(out_weight.shape)
    table_grad = table_total.reshape(speaker_table.shape)
    conv_new, conv_m_new, conv_v_new = adamw(conv_weight, conv_m, conv_v, conv_grad, 0.03)
    out_new, out_m_new, out_v_new = adamw(out_weight, out_m, out_v, out_grad, 0.1)
    table_new, table_m_new, table_v_new = adamw(speaker_table, table_m, table_v, table_grad, 0.3)
    return (
        res_out,
        skip_out,
        grad_in,
        rms_out,
        conv_grad,
        conv_new,
        conv_m_new,
        conv_v_new,
        out_grad,
        out_new,
        out_m_new,
        out_v_new,
        table_grad,
        table_new,
        table_m_new,
        table_v_new,
    )


def solution(mesh):
    in_specs = (
        P(None, "mp", "seq"),
        P(None, "mp", "seq"),
        P(None, "mp", "seq"),
        P(None, "mp", "seq"),
        P(),
        P(),
        P("section", None, None, None, "mp"),
        P("section", None, None, None, "mp"),
        P("section", None, None, None, "mp"),
        P("section", "mp", None),
        P("section", "mp", None),
        P("section", "mp", None),
        P("section", None, None, "mp"),
        P("section", None, None, "mp"),
        P("section", None, None, "mp"),
    )
    out_specs = (
        P("section", None, "mp", "seq"),
        P("section", None, "mp", "seq"),
        P("section", None, "mp", "seq"),
        P("section", None),
        P("section", None, None, None, "mp"),
        P("section", None, None, None, "mp"),
        P("section", None, None, None, "mp"),
        P("section", None, None, None, "mp"),
        P("section", "mp", None),
        P("section", "mp", None),
        P("section", "mp", None),
        P("section", "mp", None),
        P("section", None, None, "mp"),
        P("section", None, None, "mp"),
        P("section", None, None, "mp"),
        P("section", None, None, "mp"),
    )
    return jax.shard_map(shards, mesh=mesh, in_specs=in_specs, out_specs=out_specs, check_vma=False)
```

profile of v0, /device:TPU:0, one launch (start us, length us, event | category | flops | bytes accessed | tf_op | source)
XLA Modules:
  0.0 873.5 jit_solution(7935944846660688762)
XLA Ops:
  7.2 2.0 bitcast_convert_fusion
  9.2 4.9 collective-permute-start
  14.2 5.5 collective-permute-done
  20.0 2.1 pad_maximum_fusion
  25.7 31.9 %all-gather.7.cloned.1.call-done = bf16[2,512,1024]{2,1,0:T(8,128)(2,1)} async-done(((bf16[2,256,1024]{2,1,0:T(8,128)(2,1)}), bf16[2,512,1024]{2,1,0:T(8,128)(2,1)}) %all-gather.7.cloned.1.call-update) | async-done | bytes 2097168 | tf_op jit(solution)/shard_map/all_gather | solution.py:95
  57.6 2.9 add_bitcast_fusion.2
  61.0 2.8 fusion.75
  63.8 54.4 %reduce-scatter.7.cloned.1.call-done = f32[2,256,1024]{2,1,0:T(8,128)} async-done(((f32[2,512,1024]{2,1,0:T(8,128)}), f32[2,256,1024]{2,1,0:T(8,128)}) %reduce-scatter.7.cloned.1.call-update) | async-done | bytes 2097168 | tf_op jit(solution)/shard_map/reduce_scatter | solution.py:111
  119.6 1.8 collective-permute-start.1
  121.4 2.2 collective-permute-done.1
  124.8 3.4 collective-permute-start.2
  128.2 6.1 collective-permute-done.2
  136.5 33.5 %all-gather.9.cloned.1.call-done = bf16[2,512,1024]{2,1,0:T(8,128)(2,1)} async-done(((bf16[2,256,1024]{2,1,0:T(8,128)(2,1)}), bf16[2,512,1024]{2,1,0:T(8,128)(2,1)}) %all-gather.9.cloned.1.call-update) | async-done | bytes 2097168 | tf_op jit(solution)/shard_map/all_gather | solution.py:95
  169.9 2.9 add_bitcast_fusion.1
  173.3 2.8 fusion.73
  177.9 2.7 collective-permute-start.5
  182.0 48.5 %reduce-scatter.9.cloned.1.call-done = f32[2,256,1024]{2,1,0:T(8,128)} async-done(((f32[2,512,1024]{2,1,0:T(8,128)}), f32[2,256,1024]{2,1,0:T(8,128)}) %reduce-scatter.9.cloned.1.call-update) | async-done | bytes 2097168 | tf_op jit(solution)/shard_map/reduce_scatter | solution.py:111
  230.5 5.2 select_bitcast_fusion.2
  235.8 2.2 collective-permute-start.3
  238.0 2.2 collective-permute-done.3
  241.2 3.5 collective-permute-start.4
  244.8 6.1 collective-permute-done.4
  254.3 3.0 multiply_convert_fusion.2
  259.4 27.1 %all-gather.11.cloned.1.call-done = bf16[2,512,1024]{2,1,0:T(8,128)(2,1)} async-done(((bf16[2,256,1024]{2,1,0:T(8,128)(2,1)}), bf16[2,512,1024]{2,1,0:T(8,128)(2,1)}) %all-gather.11.cloned.1.call-update) | async-done | bytes 2097168 | tf_op jit(solution)/shard_map/all_gather | solution.py:95
  286.5 7.7 broadcast_select_fusion
  294.3 27.4 %all-gather.13.cloned.1.call-done = bf16[2,512,1024]{2,1,0:T(8,128)(2,1)} async-done(((bf16[2,256,1024]{2,1,0:T(8,128)(2,1)}), bf16[2,512,1024]{2,1,0:T(8,128)(2,1)}) %all-gather.13.cloned.1.call-update) | async-done | bytes 2097168 | tf_op jit(solution)/shard_map/all_gather | solution.py:173
  321.6 3.3 multiply_convert_fusion.7
  325.0 3.3 fusion.86
  328.3 54.4 %reduce-scatter.13.cloned.1.call-done = f32[2,256,1024]{2,1,0:T(8,128)} async-done(((f32[2,512,1024]{2,1,0:T(8,128)}), f32[2,256,1024]{2,1,0:T(8,128)}) %reduce-scatter.13.cloned.1.call-update) | async-done | bytes 2097168 | tf_op jit(solution)/shard_map/reduce_scatter | solution.py:191
  382.7 2.3 slice_bitcast_fusion.4
  386.4 5.8 dynamic_update_slice.9
  396.3 12.9 %collective-permute-done.7 = f32[256,512]{1,0:T(8,128)S(1)} collective-permute-done((f32[256,512]{1,0:T(8,128)S(1)}, f32[256,512]{1,0:T(8,128)S(1)}, u32[]{:S(2)}, u32[]{:S(2)}) %collective-permute-start.7) | collective-permute-done | bytes 524320 | tf_op jit(solution)/shard_map/ppermute | solution.py:22
  411.0 3.3 collective-permute-done.8
  416.6 33.2 %all-gather.15.cloned.1.call-done = bf16[2,512,1024]{2,1,0:T(8,128)(2,1)} async-done(((bf16[2,256,1024]{2,1,0:T(8,128)(2,1)}), bf16[2,512,1024]{2,1,0:T(8,128)(2,1)}) %all-gather.15.cloned.1.call-update) | async-done | bytes 2097168 | tf_op jit(solution)/shard_map/all_gather | solution.py:173
  449.8 3.3 multiply_convert_fusion.4
  453.2 3.3 fusion.85
  456.5 54.4 %reduce-scatter.15.cloned.1.call-done = f32[2,256,1024]{2,1,0:T(8,128)} async-done(((f32[2,512,1024]{2,1,0:T(8,128)}), f32[2,256,1024]{2,1,0:T(8,128)}) %reduce-scatter.15.cloned.1.call-update) | async-done | bytes 2097168 | tf_op jit(solution)/shard_map/reduce_scatter | solution.py:191
  510.9 2.3 slice_bitcast_fusion.2
  514.6 5.8 dynamic_update_slice.10
  524.6 12.9 %collective-permute-done.9 = f32[256,512]{1,0:T(8,128)S(1)} collective-permute-done((f32[256,512]{1,0:T(8,128)S(1)}, f32[256,512]{1,0:T(8,128)S(1)}, u32[]{:S(2)}, u32[]{:S(2)}) %collective-permute-start.9) | collective-permute-done | bytes 524320 | tf_op jit(solution)/shard_map/ppermute | solution.py:22
  540.6 3.3 collective-permute-done.10
  546.2 2.0 fusion.53
  548.3 2.7 fusion.71
  553.3 2.8 fusion.79
  560.1 2.6 fusion.3
  562.7 16.8 %all-gather.17.cloned.1.call-done = bf16[2,512,1024]{2,1,0:T(8,128)(2,1)} async-done(((bf16[2,256,1024]{2,1,0:T(8,128)(2,1)}), bf16[2,512,1024]{2,1,0:T(8,128)(2,1)}) %all-gather.17.cloned.1.call-update) | async-done | bytes 2097168 | tf_op jit(solution)/shard_map/all_gather | solution.py:173
  579.5 3.5 multiply_convert_fusion.1
  586.5 2.6 add_add_fusion
  589.1 3.5 reshape.337
  595.0 3.8 convolution_add_fusion
  598.8 4.5 fusion.84
  603.3 3.0 collective-permute-start.6
  607.5 1.9 fusion.99
  612.7 23.4 %reduce-scatter.11.cloned.1.call-done = f32[2,256,1024]{2,1,0:T(8,128)} async-done(((f32[2,512,1024]{2,1,0:T(8,128)}), f32[2,256,1024]{2,1,0:T(8,128)}) %reduce-scatter.11.cloned.1.call-update) | async-done | bytes 2097168 | tf_op jit(solution)/shard_map/reduce_scatter | solution.py:111
  636.1 6.7 multiply_reduce_fusion
  646.7 43.7 %all-reduce = (f32[]{:T(128)}, f32[]{:T(128)}, f32[]{:T(128)}) all-reduce(f32[]{:T(128)S(6)} %add.306, f32[]{:T(128)S(6)} %add.304, f32[]{:T(128)S(6)} %add.302), channel_id=1, replica_groups=mesh['section'=2,'seq'=8,'mp'=2] {'seq','mp'}, use_global_device_ids=true, to_apply=%region_17.18 | all-reduce | flops 3 | bytes 24 | tf_op jit(solution)/shard_map/psum | solution.py:130
  693.8 3.3 maximum_bitcast_fusion
  698.5 79.7 %all-reduce.4.cloned.1.call-done = (f32[1,2,512,2,256]{4,3,2,1,0:T(2,128)}, f32[256,1024]{1,0:T(8,128)}, f32[1,109,2,256]{3,2,1,0:T(2,128)}) async-done(((f32[1,2,512,2,256]{4,3,2,1,0:T(2,128)}, f32[256,1024]{1,0:T(8,128)}, f32[1,109,2,256]{3,2,1,0:T(2,128)}), (f32[1,2,512,2,256]{4,3,2,1,0:T(2,128)}, f32[256,1024]{1,0:T(8,128)}, f32[1,109,2,256]{3,2,1,0:T(2,128)})) %all-reduce.4.cloned.1.call-update) | async-done | bytes 3368976 | tf_op jit(solution)/shard_map/psum | solution.py:223
  778.1 4.3 multiply_subtract_fusion.1
  782.7 10.0 %multiply_subtract_fusion = (f32[1,2,512,2,256]{4,3,2,1,0:T(2,128)}, f32[1,2,512,2,256]{4,3,2,1,0:T(2,128)}, f32[1,2,512,2,256]{4,3,2,1,0:T(2,128)}) fusion(f32[1,2,512,2,256]{4,3,2,1,0:T(2,128)S(1)} %copy-done.14, f32[1,2,512,2,256]{4,3,2,1,0:T(2,128)S(1)} %copy-done.15, f32[1,2,512,2,256]{4,3,2,1,0:T(2,128)S(1)} %copy-done.42, f32[1,2,512,2,256]{4,3,2,1,0:T(2,128)} %param.29), kind=kLoop, calls=%fused_computation.8 | loop fusion | flops 7864320 | bytes 14680064 | tf_op jit(solution)/shard_map/sub | solution.py:31
  792.7 41.1 %reduce-scatter.17.cloned.1.call-done = f32[2,256,1024]{2,1,0:T(8,128)} async-done(((f32[2,512,1024]{2,1,0:T(8,128)}), f32[2,256,1024]{2,1,0:T(8,128)}) %reduce-scatter.17.cloned.1.call-update) | async-done | bytes 2097168 | tf_op jit(solution)/shard_map/reduce_scatter | solution.py:191
  836.5 5.6 dynamic_update_slice.11
  844.6 2.7 multiply_subtract_fusion.2
  848.8 10.3 %collective-permute-done.11 = f32[256,512]{1,0:T(8,128)S(1)} collective-permute-done((f32[256,512]{1,0:T(8,128)S(1)}, f32[256,512]{1,0:T(8,128)S(1)}, u32[]{:S(2)}, u32[]{:S(2)}) %collective-permute-start.11) | collective-permute-done | bytes 524320 | tf_op jit(solution)/shard_map/ppermute | solution.py:22
  (225 shorter events, 70.7 us)
Async XLA Ops:
  7.2 50.4 %all-gather.7.cloned.1.call-start = ((), (), s32[]{:S(2)}) async-start(), calls=%async_computation.6 | async-start | bytes 3145728 | tf_op jit(solution)/shard_map/all_gather | solution.py:95
  9.2 10.4 %collective-permute-start = (bf16[256,512]{1,0:T(8,128)(2,1)S(1)}, bf16[256,512]{1,0:T(8,128)(2,1)S(1)}, u32[]{:S(2)}, u32[]{:S(2)}) collective-permute-start(bf16[256,512]{1,0:T(8,128)(2,1)S(1)} %slice.235), channel_id=1, source_target_pairs={{0,2},{2,4},{4,6},{6,8},{8,10},{10,12},{12,14},{1,3},{3,5},{5,7},{... | collective-permute-start | bytes 786440 | tf_op jit(solution)/shard_map/ppermute | solution.py:22
  14.1 8.1 copy-start.13
  22.1 96.0 %reduce-scatter.7.cloned.1.call-start = ((), (), s32[]{:S(2)}) async-start(), calls=%async_computation.7 | async-start | bytes 6291456 | tf_op jit(solution)/shard_map/reduce_scatter | solution.py:111
  24.3 149.0 %copy-start.11 = (bf16[1,256,1024]{2,1,0:T(8,128)(2,1)}, bf16[1,256,1024]{2,1,0:T(8,128)(2,1)S(1)}, u32[]{:S(2)}) copy-start(bf16[1,256,1024]{2,1,0:T(8,128)(2,1)S(1)} %convert_element_type.152) | copy-start | bytes 1572868
  60.5 3.2 copy-start.9
  60.9 2.8 copy-start.3
  63.7 54.5 %copy-start.1 = (bf16[2,256,1024]{2,1,0:T(8,128)(2,1)S(1)}, bf16[2,256,1024]{2,1,0:T(8,128)(2,1)}, u32[]{:S(2)}) copy-start(bf16[2,256,1024]{2,1,0:T(8,128)(2,1)} %param.21) | copy-start | bytes 3145732
  63.7 106.2 %all-gather.9.cloned.1.call-start = ((), (), s32[]{:S(2)}) async-start(), calls=%async_computation.8 | async-start | bytes 3145728 | tf_op jit(solution)/shard_map/all_gather | solution.py:95
  119.6 5.1 copy-start.28
  119.6 4.0 collective-permute-start.1
  124.8 9.5 %collective-permute-start.2 = (bf16[256,512]{1,0:T(8,128)(2,1)S(1)}, bf16[256,512]{1,0:T(8,128)(2,1)S(1)}, u32[]{:S(2)}, u32[]{:S(2)}) collective-permute-start(bf16[256,512]{1,0:T(8,128)(2,1)S(1)} %slice.239), channel_id=1, source_target_pairs={{0,2},{2,4},{4,6},{6,8},{8,10},{10,12},{12,14},{1,3},{3,5},{5,7},{... | collective-permute-start | bytes 786440 | tf_op jit(solution)/shard_map/ppermute | solution.py:22
  135.7 94.9 %reduce-scatter.9.cloned.1.call-start = ((), (), s32[]{:S(2)}) async-start(), calls=%async_computation.9 | async-start | bytes 6291456 | tf_op jit(solution)/shard_map/reduce_scatter | solution.py:111
  172.8 3.2 copy-start.10
  176.1 4.6 copy-start.61
  176.1 110.4 %all-gather.11.cloned.1.call-start = ((), (), s32[]{:S(2)}) async-start(), calls=%async_computation.10 | async-start | bytes 3145728 | tf_op jit(solution)/shard_map/all_gather | solution.py:95
  177.9 52.7 %copy-start.32 = (f32[256,1024]{1,0:T(8,128)}, f32[256,1024]{1,0:T(8,128)S(1)}, u32[]{:S(2)}) copy-start(f32[256,1024]{1,0:T(8,128)S(1)} %fusion.30) | copy-start | bytes 3145732
  177.9 4.1 collective-permute-start.5
  235.7 4.7 copy-start.8
  235.8 4.4 collective-permute-start.3
  241.2 13.0 %copy-start = (f32[2,256,1024]{2,1,0:T(8,128)S(1)}, f32[2,256,1024]{2,1,0:T(8,128)}, u32[]{:S(2)}) copy-start(f32[2,256,1024]{2,1,0:T(8,128)} %param.23) | copy-start | bytes 6291460
  241.2 9.6 %collective-permute-start.4 = (bf16[256,512]{1,0:T(8,128)(2,1)S(1)}, bf16[256,512]{1,0:T(8,128)(2,1)S(1)}, u32[]{:S(2)}, u32[]{:S(2)}) collective-permute-start(bf16[256,512]{1,0:T(8,128)(2,1)S(1)} %slice.243), channel_id=1, source_target_pairs={{0,2},{2,4},{4,6},{6,8},{8,10},{10,12},{12,14},{1,3},{3,5},{5,7},{... | collective-permute-start | bytes 786440 | tf_op jit(solution)/shard_map/ppermute | solution.py:22
  252.2 69.4 %all-gather.13.cloned.1.call-start = ((), (), s32[]{:S(2)}) async-start(), calls=%async_computation.12 | async-start | bytes 3145728 | tf_op jit(solution)/shard_map/all_gather | solution.py:173
  258.4 124.4 %reduce-scatter.13.cloned.1.call-start = ((), (), s32[]{:S(2)}) async-start(), calls=%async_computation.13 | async-start | bytes 6291456 | tf_op jit(solution)/shard_map/reduce_scatter | solution.py:191
  325.0 3.3 copy-start.18
  325.0 3.3 copy-start.21
  328.3 121.5 %all-gather.15.cloned.1.call-start = ((), (), s32[]{:S(2)}) async-start(), calls=%async_computation.14 | async-start | bytes 3145728 | tf_op jit(solution)/shard_map/all_gather | solution.py:173
  393.3 15.9 %collective-permute-start.7 = (f32[256,512]{1,0:T(8,128)S(1)}, f32[256,512]{1,0:T(8,128)S(1)}, u32[]{:S(2)}, u32[]{:S(2)}) collective-permute-start(f32[256,512]{1,0:T(8,128)S(1)} %slice.256), channel_id=1, source_target_pairs={{2,0},{4,2},{6,4},{8,6},{10,8},{12,10},{14,12},{3,1},{5,3},{7,5},{... | collective-permute-start | bytes 1572872 | tf_op jit(solution)/shard_map/ppermute | solution.py:22
  409.6 5.9 copy-start.40
  409.6 5.9 copy-start.47
  409.6 4.7 collective-permute-start.8
  416.6 94.4 %reduce-scatter.15.cloned.1.call-start = ((), (), s32[]{:S(2)}) async-start(), calls=%async_computation.15 | async-start | bytes 6291456 | tf_op jit(solution)/shard_map/reduce_scatter | solution.py:191
  453.2 3.3 copy-start.52
  453.2 3.3 copy-start.54
  456.5 123.0 %all-gather.17.cloned.1.call-start = ((), (), s32[]{:S(2)}) async-start(), calls=%async_computation.16 | async-start | bytes 3145728 | tf_op jit(solution)/shard_map/all_gather | solution.py:173
  521.5 16.2 %copy-start.38 = (f32[256,1024]{1,0:T(8,128)S(1)}, f32[256,1024]{1,0:T(8,128)}, u32[]{:S(2)}) copy-start(f32[256,1024]{1,0:T(8,128)} %copy-done.37) | copy-start | bytes 3145732
  521.5 16.2 %copy-start.41 = (f32[256,1024]{1,0:T(8,128)S(1)}, f32[256,1024]{1,0:T(8,128)}, u32[]{:S(2)}) copy-start(f32[256,1024]{1,0:T(8,128)} %copy-done.40) | copy-start | bytes 3145732
  521.5 16.0 %collective-permute-start.9 = (f32[256,512]{1,0:T(8,128)S(1)}, f32[256,512]{1,0:T(8,128)S(1)}, u32[]{:S(2)}, u32[]{:S(2)}) collective-permute-start(f32[256,512]{1,0:T(8,128)S(1)} %slice.263), channel_id=1, source_target_pairs={{2,0},{4,2},{6,4},{8,6},{10,8},{12,10},{14,12},{3,1},{5,3},{7,5},{... | collective-permute-start | bytes 1572872 | tf_op jit(solution)/shard_map/ppermute | solution.py:22
  539.1 5.9 copy-start.34
  539.1 5.9 copy-start.46
  539.1 4.7 collective-permute-start.10
  546.2 89.9 %reduce-scatter.11.cloned.1.call-start = ((), (), s32[]{:S(2)}) async-start(), calls=%async_computation.11 | async-start | bytes 6291456 | tf_op jit(solution)/shard_map/reduce_scatter | solution.py:111
  551.1 227.1 %all-reduce.4.cloned.1.call-start = ((), (), s32[]{:S(2)}) async-start(), calls=%async_computation.18 | async-start | bytes 6737920 | tf_op jit(solution)/shard_map/psum | solution.py:223
  553.2 2.9 copy-start.19
  553.2 2.9 copy-start.22
  553.2 3.1 copy-start.53
  553.3 3.1 copy-start.55
  553.3 3.5 copy-start.45
  579.5 4.5 copy-start.44
  579.5 4.5 copy-start.50
  598.8 235.1 %reduce-scatter.17.cloned.1.call-start = ((), (), s32[]{:S(2)}) async-start(), calls=%async_computation.17 | async-start | bytes 6291456 | tf_op jit(solution)/shard_map/reduce_scatter | solution.py:191
  603.3 32.8 %copy-start.2 = (bf16[2,256,1024]{2,1,0:T(8,128)(2,1)S(1)}, bf16[2,256,1024]{2,1,0:T(8,128)(2,1)}, u32[]{:S(2)}) copy-start(bf16[2,256,1024]{2,1,0:T(8,128)(2,1)} %param.21) | copy-start | bytes 3145732
  603.3 9.4 %collective-permute-start.6 = (f32[256,1024]{1,0:T(8,128)}, f32[256,1024]{1,0:T(8,128)}, u32[]{:S(2)}, u32[]{:S(2)}) collective-permute-start(f32[256,1024]{1,0:T(8,128)} %get-tuple-element.78), channel_id=1, source_target_pairs={{0,16},{1,17},{2,18},{3,19},{4,20},{5,21},{6,22},{7,23},{8,24},{9,... | collective-permute-start | bytes 3145736 | tf_op jit(solution)/shard_map/ppermute | solution.py:22
  693.7 3.3 copy-start.33
  693.7 3.3 copy-start.36
  697.0 81.1 %copy-start.27 = (f32[1,256,1024]{2,1,0:T(8,128)S(1)}, f32[1,256,1024]{2,1,0:T(8,128)}, u32[]{:S(2)}) copy-start(f32[1,256,1024]{2,1,0:T(8,128)} %param.30) | copy-start | bytes 3145732
  778.1 4.3 copy-start.14
  778.1 4.3 copy-start.15
  778.1 4.5 copy-start.42
  835.2 9.4 %copy-start.58 = (f32[1,109,2,256]{3,2,1,0:T(2,128)S(1)}, f32[1,109,2,256]{3,2,1,0:T(2,128)}, u32[]{:S(2)}) copy-start(f32[1,109,2,256]{3,2,1,0:T(2,128)} %get-tuple-element.133) | copy-start | bytes 669700
  842.1 5.2 copy-start.17
  843.3 15.9 %collective-permute-start.11 = (f32[256,512]{1,0:T(8,128)S(1)}, f32[256,512]{1,0:T(8,128)S(1)}, u32[]{:S(2)}, u32[]{:S(2)}) collective-permute-start(f32[256,512]{1,0:T(8,128)S(1)} %slice.270), channel_id=1, source_target_pairs={{2,0},{4,2},{6,4},{8,6},{10,8},{12,10},{14,12},{3,1},{5,3},{7,5},{... | collective-permute-start | bytes 1572872 | tf_op jit(solution)/shard_map/ppermute | solution.py:22
  847.3 12.0 %copy-start.30 = (f32[256,1024]{1,0:T(8,128)S(1)}, f32[256,1024]{1,0:T(8,128)}, u32[]{:S(2)}) copy-start(f32[256,1024]{1,0:T(8,128)} %copy-done.29) | copy-start | bytes 3145732
  847.3 12.0 %copy-start.35 = (f32[256,1024]{1,0:T(8,128)S(1)}, f32[256,1024]{1,0:T(8,128)}, u32[]{:S(2)}) copy-start(f32[256,1024]{1,0:T(8,128)} %copy-done.34) | copy-start | bytes 3145732
  (23 other events, 36.3 us)
Sparse Core Ops, SparseCore 0:
  22.3 35.3 all-gather.6
  63.9 54.2 reduce-scatter.6
  135.8 34.1 all-gather.8
  176.2 54.3 reduce-scatter.8
  252.4 34.1 all-gather.10
  288.5 33.1 all-gather.12
  328.4 54.2 reduce-scatter.12
  416.7 33.0 all-gather.14
  456.6 54.3 reduce-scatter.14
  546.3 33.1 all-gather.16
  581.8 54.2 reduce-scatter.10
  641.5 136.5 all-reduce.3
  780.4 53.3 reduce-scatter.16
where the time goes:
time: 883 us; the launch traced here: 873 us
  waiting for transfers between devices  591 us (67%)
  other arithmetic  75.2 us (9%)
  matrix products  59.9 us (7%)
  local copies, waits for them, and re-layouts  50.7 us (6%)
  blocking collectives  43.7 us (5%)
  starting transfers between devices  29.3 us (3%)
  between operations  23.9 us (3%)
    reduce_scatter x3, waiting for transfers between devices, shards(): lax.psum_scatter(tap_terms.reshape(2, full_res, block_length_rows), 'mp',...  150 us
    reduce_scatter x3, waiting for transfers between devices, shards(): lax.psum_scatter(partial_sums, 'mp', scatter_dimension=1, tiled=True)  126 us
    all_gather x3, waiting for transfers between devices, shards(): lax.all_gather(tap_rows, 'mp', axis=1, tiled=True)  92.5 us
    psum x1, waiting for transfers between devices, shards(): lax.psum((conv_acc, out_acc, table_acc), 'seq')  79.7 us
    all_gather x3, waiting for transfers between devices, shards(): lax.all_gather(proj_grad, 'mp', axis=1, tiled=True)  77.4 us
    ppermute x12, waiting for transfers between devices, passed_along(): lax.ppermute(value, axis, [(source, source + steps) for source in range(f...  64.9 us
    psum x1, blocking collectives, shards(): lax.psum((square_res, square_branch, counted), ('seq', 'mp'))  43.7 us
    ppermute x12, starting transfers between devices, passed_along(): lax.ppermute(value, axis, [(source, source + steps) for source in range(f...  28.4 us
  transfers between devices with their start and end apart: 25, of which 24 were waited for; matrix products, arithmetic and copies ran while one was open for 11% of the time, Pallas kernels for 0%

commit v1 on v0

--- a/solution.py
+++ b/solution.py
@@ -1,13 +1,19 @@
+import functools
 import math
 
 import jax
 import jax.numpy as jnp
 from jax import lax
+from jax.experimental import pallas as pl
+from jax.experimental.pallas import tpu as pltpu
 from jax.sharding import PartitionSpec as P
 
 FIRST_DILATION = 512
 STEP = 10
-
+MESH = pl.DeviceIdType.MESH
+TILE = 256
+UNITS = 6
+Z_FIRST = 3
 
 beta_one = 0.9
 beta_two = 0.999
@@ -30,6 +36,1097 @@
     update = moment_new / corr_one / (jnp.sqrt(second_new / corr_two) + adam_eps)
     weight_new = weight - step_rate * (update + decay_rate * weight)
     return (weight_new, moment_new, second_new)
+
+
+def dot(left, right):
+    return jnp.dot(left, right, preferred_element_type=jnp.float32)
+
+
+def dot_last(left, right):
+    return lax.dot_general(
+        left, right, (((1,), (1,)), ((), ())), preferred_element_type=jnp.float32
+    )
+
+
+def rows_at(start, size):
+    return pl.ds(start if isinstance(start, int) else pl.multiple_of(start, 16), size)
+
+
+def cols_at(start, size):
+    return pl.ds(start if isinstance(start, int) else pl.multiple_of(start, 128), size)
+
+
+def layers_kernel(
+    sizes,
+    x_ref,
+    skip_ref,
+    cot_res_ref,
+    cot_skip_ref,
+    lengths_ref,
+    speakers_ref,
+    conv_ref,
+    out_ref,
+    table_ref,
+    res_ref,
+    skipped_ref,
+    grad_ref,
+    weight_ref,
+    small_ref,
+    conv_wide,
+    out_wide,
+    table_wide,
+    xf,
+    wc,
+    wct,
+    wo,
+    wot,
+    et,
+    in1,
+    next_out,
+    next_in,
+    past1,
+    act_f,
+    act_q,
+    hid,
+    dproj,
+    dres0,
+    dpre,
+    grad1,
+    past_grad1,
+    edge_out,
+    edge_in,
+    res0,
+    skip_sum,
+    cot_a,
+    cot_b,
+    skip_low,
+    res_low,
+    grad1_low,
+    grad0,
+    past0_out,
+    past0_in,
+    grad0_low,
+    stats,
+    acc,
+    from_core,
+    down,
+    final,
+    small,
+    small_in,
+    small_sum,
+    send_sem,
+    recv_sem,
+    local_sem,
+):
+    full, local, gates, span, n_seq = sizes
+    gate_local = gates // 2
+    width = 2 * gate_local
+    halo = FIRST_DILATION
+    n_z = n_seq // 2
+    c = lax.axis_index("section")
+    s = lax.axis_index("seq")
+    x = lax.axis_index("mp")
+    z, y = s // 2, s % 2
+    oc, ox = 1 - c, 1 - x
+    bf16, f32 = jnp.bfloat16, jnp.float32
+    counts = {"send": 0, "recv": 0, "local": 0}
+    pending = []
+    inside = [None]
+
+    def take(kind, amount=1):
+        counts[kind] += amount
+        return counts[kind] - amount
+
+    def when(cond, action):
+        if cond is None:
+            action()
+        else:
+            pl.when(cond)(action)
+
+    def on(cond, action):
+        inside[0] = cond
+        pl.when(cond)(lambda: action())
+        inside[0] = None
+
+    def send(source, target, device, recv_at, cond=None):
+        at = take("send")
+
+        def make():
+            return pltpu.make_async_remote_copy(
+                src_ref=source(),
+                dst_ref=target(),
+                send_sem=send_sem.at[at],
+                recv_sem=recv_sem.at[recv_at()],
+                device_id=device(),
+                device_id_type=MESH,
+            )
+
+        when(cond, lambda: make().start())
+        pending.append((lambda: make().wait_send(), inside[0] if cond is None else cond))
+
+    def arrive(target, recv_at, cond=None):
+        when(
+            cond,
+            lambda: pltpu.make_async_remote_copy(
+                src_ref=target,
+                dst_ref=target,
+                send_sem=send_sem.at[0],
+                recv_sem=recv_sem.at[recv_at],
+                device_id={"section": oc},
+                device_id_type=MESH,
+            ).wait_recv(),
+        )
+
+    def fetch(source, target, cond=None):
+        copy = pltpu.make_async_copy(source, target, local_sem.at[take("local")])
+        when(cond, copy.start)
+        return copy
+
+    def to(axis, index):
+        return lambda: {axis: index()}
+
+    core_dev = to("section", lambda: 1 - c)
+    mp_dev = to("mp", lambda: 1 - x)
+    y_dev = to("seq", lambda: z * 2 + 1 - y)
+    prev_dev, next_dev = to("seq", lambda: s - 1), to("seq", lambda: s + 1)
+    has_prev, has_next = s > 0, s < n_seq - 1
+
+    z_seqs = [lax.rem(z + step, n_z) * 2 + y for step in range(n_z)]
+
+    def z_seq(step):
+        return z_seqs[step]
+
+    def z_dev(step):
+        return to("seq", lambda: z_seq(step))
+
+    bits = [y] + [(z // (1 << bit)) % 2 for bit in range((n_seq // 2).bit_length() - 1)]
+    pairs = [z * 2 + 1 - y] + [
+        (z + (1 - 2 * bits[bit + 1]) * (1 << bit)) * 2 + y for bit in range(len(bits) - 1)
+    ]
+    depth = len(bits)
+    pair_devs = [to("seq", lambda way=way: pairs[way]) for way in range(depth)]
+
+    barrier = pltpu.get_barrier_semaphore()
+    for device in [core_dev, mp_dev, y_dev, *[z_dev(step) for step in range(1, n_z)]]:
+        pl.semaphore_signal(barrier, inc=1, device_id=device(), device_id_type=MESH)
+    before, after = (y == 0) & (z > 0), (y == 1) & (z < n_z - 1)
+
+    @pl.when(before)
+    def _():
+        pl.semaphore_signal(barrier, inc=1, device_id=prev_dev(), device_id_type=MESH)
+
+    @pl.when(after)
+    def _():
+        pl.semaphore_signal(barrier, inc=1, device_id=next_dev(), device_id_type=MESH)
+
+    own_rows, other_rows = rows_at(x * local, local), rows_at(ox * local, local)
+    got_conv = fetch(conv_ref, conv_wide)
+    got_table = fetch(table_ref, table_wide)
+    got_out = fetch(out_ref, out_wide)
+    got_cot_a = fetch(cot_res_ref.at[c], cot_a)
+    got_cot_b = fetch(cot_skip_ref.at[c], cot_b)
+    chunks = span // halo
+    got_x = [
+        fetch(x_ref.at[c, :, pl.ds(chunk * halo, halo)], xf.at[chunk + 1, own_rows])
+        for chunk in range(chunks)
+    ]
+    got_skip = fetch(skip_ref.at[c], skip_sum)
+
+    def cast_conv(step, carry):
+        for block in range(width // 128):
+            half, lane = block // (gate_local // 128), block % (gate_local // 128)
+            first = step * 256 * (width // 128) + lane * 2 + half
+            wc[c, x, rows_at(step * 256, 256), pl.ds(block * 128, 128)] = conv_wide[
+                pl.ds(first, 256, stride=width // 128), :
+            ].astype(bf16)
+        return carry
+
+    got_conv.wait()
+    lax.fori_loop(0, 2 * full // 256, cast_conv, None)
+    got_table.wait()
+    marks = lax.broadcasted_iota(jnp.int32, (16, width), 0)
+    emb = jnp.zeros((16, width), f32)
+    for micro in range(2):
+        rows = table_wide[speakers_ref[micro]]
+        row = jnp.concatenate([rows[0:1, :], rows[1:2, :]], axis=1)
+        emb = jnp.where(marks == micro, row, emb)
+    wc[c, x, 2 * full : 2 * full + 16, :] = emb.astype(bf16)
+    got_out.wait()
+    wo[c, rows_at(x * gate_local, gate_local), :] = out_wide[...].astype(bf16)
+
+    @pl.when(before | after)
+    def _():
+        pl.semaphore_wait(barrier, 3 + n_z)
+
+    @pl.when(jnp.logical_not(before | after))
+    def _():
+        pl.semaphore_wait(barrier, 2 + n_z)
+
+    conv_rows, out_rows = 2 * full // n_seq, gate_local // n_seq
+    conv_at, conv_core_at = take("recv", n_seq), take("recv", n_seq)
+    out_at, emb_at = take("recv", n_seq), take("recv")
+
+    def conv_slice(index, layer, block):
+        return wc.at[layer, block, rows_at(index * conv_rows, conv_rows)]
+
+    def out_slice(index, layer, block):
+        return wo.at[layer, rows_at(block * gate_local + index * out_rows, out_rows)]
+
+    def emb_part(layer, block):
+        return wc.at[layer, block, 2 * full : 2 * full + 16]
+
+    def conv_block(layer, block):
+        return wc.at[layer, block, 0 : 2 * full]
+
+    def out_block(layer, block):
+        return wo.at[layer, rows_at(block * gate_local, gate_local)]
+
+    def send_same(ref, device, recv_at, cond=None):
+        send(ref, ref, device, recv_at, cond)
+
+    def cross_weights():
+        send_same(lambda: conv_slice(s, c, x), mp_dev, lambda: conv_at + s)
+        send_same(lambda: emb_part(c, x), mp_dev, lambda: emb_at)
+        send_same(lambda: out_slice(s, c, x), mp_dev, lambda: out_at + s)
+
+    on(c == 0, cross_weights)
+    x_at = [take("recv") for _ in range(chunks)]
+    for copy in got_x:
+        copy.wait()
+    for chunk in reversed(range(chunks)):
+        send_same(
+            lambda chunk=chunk: xf.at[chunk + 1, own_rows], mp_dev, lambda chunk=chunk: x_at[chunk]
+        )
+    on(c == 1, cross_weights)
+    halo_at = [take("recv"), take("recv")]
+    send(
+        lambda: xf.at[chunks, own_rows],
+        lambda: xf.at[0, own_rows],
+        next_dev,
+        lambda: halo_at[0],
+        has_next,
+    )
+    core_at = [take("recv") for _ in range(5)]
+    send_same(lambda: conv_block(c, x), core_dev, lambda: core_at[0])
+    send_same(lambda: emb_part(c, x), core_dev, lambda: core_at[1])
+    send_same(lambda: out_block(c, x), core_dev, lambda: core_at[2])
+
+    @pl.when(s == 0)
+    def _():
+        xf[0] = jnp.zeros((full, halo), bf16)
+        next_in[...] = jnp.zeros(next_in.shape, bf16)
+
+    @pl.when(s == n_seq - 1)
+    def _():
+        past0_in[...] = jnp.zeros(past0_in.shape, bf16)
+        edge_in[...] = jnp.zeros(edge_in.shape, bf16)
+
+    stats[...] = jnp.zeros(stats.shape, f32)
+    length = lengths_ref[c]
+
+    def valid_at(start, size):
+        at = s * span + start + lax.broadcasted_iota(jnp.int32, (1, size), 1)
+        return jnp.where(at < length, 1.0, 0.0).astype(f32)
+
+    def cast_cotangents(step, carry):
+        at = cols_at(step * TILE, TILE)
+        valid = valid_at(step * TILE, TILE)
+        dproj[step, own_rows, :] = (cot_a[:, at] * valid * root_half).astype(bf16)
+        dproj[step, rows_at(full + x * local, local), :] = (cot_b[:, at] * valid).astype(bf16)
+        return carry
+
+    tiles = span // TILE
+    got_cot_a.wait()
+    got_cot_b.wait()
+    lax.fori_loop(0, tiles, cast_cotangents, None)
+    cot_at = take("recv", 2 * tiles)
+
+    def cot_piece(tile, part, block):
+        return dproj.at[tile, rows_at(part * full + block * local, local)]
+
+    for tile in range(tiles):
+        for part in range(2):
+            send_same(
+                functools.partial(cot_piece, tile, part, x),
+                mp_dev,
+                lambda tile=tile, part=part: cot_at + tile * 2 + part,
+            )
+
+    def turn_conv(layer, block, first, rows):
+        wct[layer, rows_at(block * width, width), cols_at(first, rows)] = wc[
+            layer, block, rows_at(first, rows), :
+        ].T
+
+    def turn_rest(layer, block):
+        values = wc[layer, block, 2 * full : 2 * full + 16, :].astype(f32)
+        mark_row = lax.broadcasted_iota(jnp.int32, values.shape, 0)
+        picked = jnp.sum(jnp.where(mark_row == c, values, 0.0), axis=0, keepdims=True)
+        et[layer, rows_at(block * width, width), :] = jnp.broadcast_to(picked, (128, width)).T
+
+        for part, start in enumerate((x * local, full + x * local, ox * local)):
+            wot[layer, part * local : (part + 1) * local, cols_at(block * gate_local, gate_local)] = wo[
+                layer, rows_at(block * gate_local, gate_local), cols_at(start, local)
+            ].T
+
+    def turn_all(layer, block):
+        for step in range(2 * full // TILE):
+            turn_conv(layer, block, step * TILE, TILE)
+        turn_rest(layer, block)
+
+    def spread_first():
+        arrive(conv_slice(s, c, ox), conv_at + s)
+        for step in range(1, n_z):
+            send_same(lambda: conv_slice(s, c, ox), z_dev(step), lambda: conv_at + s)
+        send_same(lambda: conv_slice(s, c, ox), y_dev, lambda: conv_at + s)
+        send_same(lambda: conv_slice(s, c, ox), core_dev, lambda: conv_core_at + s)
+        arrive(emb_part(c, ox), emb_at)
+        send_same(lambda: emb_part(c, ox), core_dev, lambda: core_at[3])
+        arrive(out_slice(s, c, ox), out_at + s)
+        for step in range(1, n_z):
+            send_same(lambda: out_slice(s, c, ox), z_dev(step), lambda: out_at + s)
+        send_same(lambda: out_slice(s, c, ox), y_dev, lambda: out_at + s)
+
+    def spread_conv():
+        for step in range(1, n_z):
+            arrive(conv_slice(z_seq(step), c, ox), conv_at + z_seq(step))
+            here = functools.partial(lambda step: conv_slice(z_seq(step), c, ox), step)
+            send_same(here, y_dev, lambda step=step: conv_at + z_seq(step))
+            send_same(here, core_dev, lambda step=step: conv_core_at + z_seq(step))
+
+    def spread_out():
+        for step in range(1, n_z):
+            arrive(out_slice(z_seq(step), c, ox), out_at + z_seq(step))
+            here = functools.partial(lambda step: out_slice(z_seq(step), c, ox), step)
+            send_same(here, y_dev, lambda step=step: out_at + z_seq(step))
+
+    def spread_last():
+        for step in range(n_z):
+            arrive(conv_slice(z_seq(step) + 1 - 2 * y, c, ox), conv_at + z_seq(step) + 1 - 2 * y)
+            here = functools.partial(
+                lambda step: conv_slice(z_seq(step) + 1 - 2 * y, c, ox), step
+            )
+            send_same(here, core_dev, lambda step=step: conv_core_at + z_seq(step) + 1 - 2 * y)
+        for step in range(n_z):
+            arrive(out_slice(z_seq(step) + 1 - 2 * y, c, ox), out_at + z_seq(step) + 1 - 2 * y)
+        send_same(lambda: out_block(c, ox), core_dev, lambda: core_at[4])
+
+    def all_from_core():
+        for step in range(n_seq):
+            arrive(conv_slice(step, oc, ox), conv_core_at + step)
+        arrive(emb_part(oc, ox), core_at[3])
+        arrive(out_block(oc, ox), core_at[4])
+
+    on(c == 0, spread_first)
+
+    @pl.when(c == 0)
+    def _():
+        turn_all(0, x)
+
+    arrive(xf.at[chunks, other_rows], x_at[chunks - 1])
+    send(
+        lambda: xf.at[chunks, other_rows],
+        lambda: xf.at[0, other_rows],
+        next_dev,
+        lambda: halo_at[1],
+        has_next,
+    )
+    on(c == 0, spread_conv)
+    arrive(conv_block(oc, x), core_at[0])
+    arrive(emb_part(oc, x), core_at[1])
+    arrive(out_block(oc, x), core_at[2])
+
+    @pl.when(c == 1)
+    def _():
+        turn_all(0, x)
+
+    on(c == 0, spread_out)
+    on(c == 0, spread_last)
+
+    on(c == 1, all_from_core)
+    turn_all(0, ox)
+
+    def fold(values):
+        total = jnp.sum(values.reshape(local // 8, 8, TILE), axis=0)
+        return sum(total[:, part * 128 : (part + 1) * 128] for part in range(TILE // 128))
+
+    def gated(layer, pre, at):
+        halves = []
+        for block in range(2):
+            base = block * width
+            shift = et[layer, base : base + width, :]
+            shift = jnp.concatenate([shift] * (TILE // 128), axis=1)
+            f = jnp.tanh(pre[base : base + gate_local] + shift[:gate_local])
+            q = 0.5 * jnp.tanh(
+                0.5 * (pre[base + gate_local : base + width] + shift[gate_local:])
+            ) + 0.5
+            rows = slice(block * gate_local, (block + 1) * gate_local)
+            act_f[layer, rows, at] = f
+            act_q[layer, rows, at] = q
+            halves.append((f * q).astype(bf16))
+            hid[layer, rows, at] = halves[-1]
+        return jnp.concatenate(halves, axis=0)
+
+    def forward0(step):
+        start = step * TILE
+        at = cols_at(start, TILE)
+        chunk, inner = start // halo, pl.ds(start % halo, TILE)
+        pre = dot(wct[0], jnp.concatenate([xf[chunk, :, inner], xf[chunk + 1, :, inner]], axis=0))
+        hidden = gated(0, pre, at)
+        valid = valid_at(start, TILE)
+        proj = dot(wot[0], hidden)
+        branch = proj[0:local]
+        res = (xf[chunk + 1, own_rows, inner].astype(f32) + branch) * root_half
+        res0[:, at] = res
+        in1[own_rows, at] = res.astype(bf16)
+        stats[0, 0] += fold(valid * res * res)
+        stats[0, 1] += fold(valid * branch * branch)
+        res = (xf[chunk + 1, other_rows, inner].astype(f32) + proj[2 * local :]) * root_half
+        in1[other_rows, at] = res.astype(bf16)
+        total = skip_sum[:, at] + proj[local : 2 * local]
+        skip_sum[:, at] = total
+        skip_low[0, :, at] = total.astype(bf16)
+
+    late_tiles = (span - halo) // TILE
+    got_skip.wait()
+    for chunk in range(chunks - 1):
+        arrive(xf.at[chunk + 1, other_rows], x_at[chunk])
+    on(c == 1, spread_first)
+    for step in range(late_tiles, tiles):
+        forward0(step)
+    in1_at = take("recv")
+    next_out[...] = in1[:, span - 128 : span]
+    send(
+        lambda: next_out,
+        lambda: next_in,
+        next_dev,
+        lambda: in1_at,
+        has_next,
+    )
+    on(c == 1, spread_conv)
+    on(c == 1, spread_out)
+    arrive(xf.at[0, own_rows], halo_at[0], has_prev)
+    arrive(xf.at[0, other_rows], halo_at[1], has_prev)
+    for step in range(late_tiles):
+        forward0(step)
+    on(c == 1, spread_last)
+
+    result_at = [take("recv") for _ in range(3)]
+    locals_pending = []
+
+    def give(layer, kind, source, target):
+        copy = fetch(source, target.at[c], c == layer)
+        locals_pending.append((copy, c == layer))
+        send(lambda: source, lambda: target.at[c], core_dev, lambda: result_at[kind], c != layer)
+
+    give(0, 0, in1.at[own_rows], res_ref)
+    give(0, 1, skip_low.at[0], skipped_ref)
+
+    turn_all(1, x)
+    on(c == 0, all_from_core)
+    turn_all(1, ox)
+
+    def forward1(step):
+        start = step * TILE
+        at = cols_at(start, TILE)
+        for base in range(0, full, 256):
+            rows = slice(base, base + 256)
+            if start == 0:
+                wide = jnp.concatenate([next_in[rows, :], in1[rows, 0:TILE]], axis=1).astype(f32)
+            else:
+                wide = in1[rows, start - 128 : start + TILE].astype(f32)
+            past1[base : base + 256, at] = pltpu.roll(wide, 1, 1)[:, 128:].astype(bf16)
+        pre = dot(wct[1], jnp.concatenate([past1[:, at], in1[:, at]], axis=0))
+        hidden = gated(1, pre, at)
+        valid = valid_at(start, TILE)
+        proj = dot(wot[1, 0 : 2 * local], hidden)
+        branch = proj[0:local]
+        res = (res0[:, at] + branch) * root_half
+        res_low[:, at] = res.astype(bf16)
+        stats[1, 0] += fold(valid * res * res)
+        stats[1, 1] += fold(valid * branch * branch)
+        total = skip_sum[:, at] + proj[local:]
+        skip_low[1, :, at] = total.astype(bf16)
+
+    arrive(next_in, in1_at, has_prev)
+    for step in range(tiles):
+        forward1(step)
+    give(1, 0, res_low, res_ref)
+    give(1, 1, skip_low.at[1], skipped_ref)
+
+    def through_gates(layer, dhidden, at):
+        for block in range(2):
+            rows = slice(block * gate_local, (block + 1) * gate_local)
+            f, q = act_f[layer, rows, at], act_q[layer, rows, at]
+            d = dhidden[rows] * q
+            base = block * width
+            dpre[layer, base : base + gate_local, at] = (d * (1.0 - f * f)).astype(bf16)
+            dpre[layer, base + gate_local : base + width, at] = (d * f * (1.0 - q)).astype(bf16)
+
+    def backward1(step):
+        at = cols_at(step * TILE, TILE)
+        through_gates(1, dot(wo[1], dproj[step]), at)
+        both = jnp.concatenate([wc[1, block, 0 : 2 * full, :] for block in range(2)], axis=1)
+        taps = dot(both, dpre[1, :, at])
+        past_grad1[:, at] = taps[0:full]
+        grad1[:, at] = taps[full:] + dproj[step, 0:full, :].astype(f32)
+
+    def join1(step):
+        start = step * TILE
+        at = cols_at(start, TILE)
+        for base in range(0, full, 256):
+            rows = slice(base, base + 256)
+            wide = past_grad1[rows, cols_at(start, TILE + 128)]
+            total = grad1[rows, at] + pltpu.roll(wide, TILE + 127, 1)[:, 0:TILE]
+            grad1[rows, at] = total
+            dres0[rows, at] = (root_half * total).astype(bf16)
+        own = grad1[own_rows, at]
+        grad1_low[:, at] = own.astype(bf16)
+        grad0[:, at] = root_half * own
+
+    def backward0(step):
+        start = step * TILE
+        at = cols_at(start, TILE)
+        dhidden = dot(wo[0], jnp.concatenate([dres0[:, at], dproj[step, full:, :]], axis=0))
+        through_gates(0, dhidden, at)
+        own = [
+            jnp.concatenate([wc[0, block, rows, :] for block in range(2)], axis=1)
+            for rows in (own_rows, rows_at(full + x * local, local))
+        ]
+        taps = dot(jnp.concatenate(own, axis=0), dpre[0, :, at])
+        grad0[:, at] += taps[local:]
+        return taps[0:local]
+
+    edge_at, past0_at = take("recv"), take("recv")
+    early_tiles = halo // TILE
+
+    for step in range(tiles):
+        for part in range(2):
+            arrive(cot_piece(step, part, ox), cot_at + step * 2 + part)
+        tile = step - (tiles - early_tiles)
+        if tile >= 0:
+            join1(tile)
+        backward1(step)
+        if tile >= 0:
+            past0_out[:, cols_at(tile * TILE, TILE)] = backward0(tile).astype(bf16)
+        if step == 0:
+            edge_out[...] = past_grad1[:, 0:128].astype(bf16)
+            send(lambda: edge_out, lambda: edge_in, prev_dev, lambda: edge_at, has_prev)
+    send(lambda: past0_out, lambda: past0_in, prev_dev, lambda: past0_at, has_prev)
+
+    total_rows = 3 * full
+    unit_rows = total_rows // UNITS
+    unit_core_at = [take("recv") for _ in range(UNITS)]
+    down_at = [[take("recv") for _ in range(depth)] for _ in range(UNITS)]
+    up_at = [[take("recv") for _ in range(depth)] for _ in range(UNITS)]
+    small_at = [take("recv") for _ in range(2 + depth)]
+    stored_at = take("local", UNITS + 1)
+
+    def to_core(layer, first, size):
+        for unit in range(first // unit_rows, (first + size) // unit_rows):
+            rows = pl.ds(unit * unit_rows, unit_rows)
+            send(
+                lambda rows=rows: acc.at[layer, rows],
+                lambda rows=rows: from_core.at[rows],
+                core_dev,
+                lambda unit=unit: unit_core_at[unit],
+                c != layer,
+            )
+
+    def unit_conv(layer, past, now):
+        taps = jnp.concatenate([past, now, jnp.ones((16, span), bf16)], axis=0)
+        product = dot_last(taps, dpre[layer, rows_at(x * width, width), :])
+        acc[layer, 0 : 2 * full, :] = product[0 : 2 * full].astype(bf16)
+        sums = product[2 * full : 2 * full + 8]
+        mark = lax.broadcasted_iota(jnp.int32, sums.shape, 0)
+        small[layer, 0:8, :] = jnp.where(mark == c, sums, 0.0)
+        small[layer, 8:16, :] = jnp.zeros((8, width), f32)
+        small[layer, 8:16, 0:128] = stats[layer, 0]
+        small[layer, 8:16, 128:256] = stats[layer, 1]
+        to_core(layer, 0, 2 * full)
+        send(
+            lambda: small.at[layer],
+            lambda: small_in.at[0],
+            core_dev,
+            lambda: small_at[0],
+            c != layer,
+        )
+
+    def unit_out(layer, parts):
+        hidden = hid[layer, rows_at(x * gate_local, gate_local), :]
+        product = dot_last(jnp.concatenate(parts, axis=0), hidden)
+        for part in range(2):
+            acc[layer, pl.ds(2 * full, full), pl.ds(part * gate_local, gate_local)] = product[
+                part * full : (part + 1) * full
+            ].astype(bf16)
+        to_core(layer, 2 * full, full)
+
+    n_stages = 2 * depth + 1
+
+    def order(unit):
+        ways = list(range(depth))
+        return [1, 0, *ways[2:]] if unit == Z_FIRST and depth > 1 else ways
+
+    def kept(unit, level, flip=False):
+        start, size = unit * unit_rows, unit_rows
+        for step in range(level):
+            size //= 2
+            bit = bits[order(unit)[step]]
+            if flip and step == level - 1:
+                bit = 1 - bit
+            start = start + bit * size
+        return rows_at(start, size)
+
+    def landing(unit, level):
+        size = unit_rows >> level
+        return pl.ds(unit * unit_rows + unit_rows - 2 * size, size)
+
+    def unit_stage(layer, unit, stage):
+        ways = order(unit)
+        if stage <= depth:
+            here = kept(unit, stage)
+            if stage == 0:
+                arrive(from_core.at[here], unit_core_at[unit])
+                other = from_core[here, :]
+            else:
+                place = landing(unit, stage)
+                arrive(down.at[place], down_at[unit][stage - 1])
+                other = down[place, :]
+            total = (acc[layer, here, :].astype(f32) + other.astype(f32)).astype(bf16)
+            if stage < depth:
+                acc[layer, here, :] = total
+                send(
+                    lambda: acc.at[layer, kept(unit, stage + 1, True)],
+                    lambda: down.at[landing(unit, stage + 1)],
+                    pair_devs[ways[stage]],
+                    lambda: down_at[unit][stage],
+                )
+                return
+            final[here, :] = total
+        if stage > depth:
+            level = 2 * depth + 1 - stage
+            arrive(final.at[kept(unit, level, True)], up_at[unit][level - 1])
+        level = 2 * depth - stage
+        if level > 0:
+            send_same(
+                lambda: final.at[kept(unit, level)],
+                pair_devs[ways[level - 1]],
+                lambda: up_at[unit][level - 1],
+            )
+        else:
+            here = pl.ds(unit * unit_rows, unit_rows)
+            pltpu.make_async_copy(
+                final.at[here], weight_ref.at[here], local_sem.at[stored_at + unit]
+            ).start()
+
+    def small_stage(layer, stage):
+        names = [core_dev, mp_dev, *pair_devs]
+        arrive(small_in.at[stage], small_at[stage])
+        if stage == 0:
+            small_sum[0] = small[layer] + small_in[0]
+        else:
+            sums = small_sum[stage - 1, 0:8, :]
+            small_sum[stage, 0:8, :] = sums if stage == 1 else sums + small_in[stage, 0:8, :]
+            small_sum[stage, 8:16, :] = small_sum[stage - 1, 8:16, :] + small_in[stage, 8:16, :]
+        if stage < len(names) - 1:
+            send(
+                lambda: small_sum.at[stage],
+                lambda: small_in.at[stage + 1],
+                names[stage + 1],
+                lambda: small_at[stage + 1],
+            )
+        else:
+            pltpu.make_async_copy(
+                small_sum.at[stage], small_ref, local_sem.at[stored_at + UNITS]
+            ).start()
+
+    def in_order_of_arrival(layer, first_stage, units):
+        ready = [(float(at), at, unit, first_stage) for at, unit in enumerate(units)]
+        free = [0.0] * depth
+        clock, small_next = 0.0, 0
+        while ready:
+            ready.sort()
+            at, rank, unit, stage = ready.pop(0)
+            unit_stage(layer, unit, stage)
+            clock = max(clock, at) + 0.25
+            if stage < n_stages - 1:
+                way = order(unit)[min(stage, 2 * depth - 1 - stage)]
+                level = min(stage, 2 * depth - 1 - stage)
+                free[way] = max(free[way], clock) + 3.0 / 2**level * (2 if way == 2 else 1)
+                ready.append((free[way] + 1.0, rank, unit, stage + 1))
+            if stage == n_stages - 1 or stage == 2:
+                if small_next < 2 + depth:
+                    small_stage(layer, small_next)
+                    small_next += 1
+        for stage in range(small_next, 2 + depth):
+            small_stage(layer, stage)
+
+    unit_order = [4, 5, 0, 1, 2, 3]
+
+    def all_times(first):
+        rows = slice(first, first + full)
+        return jnp.concatenate([dproj[tile, rows, :] for tile in range(tiles)], axis=1)
+
+    unit_out(1, [all_times(0), all_times(full)])
+    unit_conv(1, past1[...], in1[...])
+
+    arrive(edge_in, edge_at, has_next)
+    past_grad1[:, span : span + 128] = edge_in[...].astype(f32)
+
+    def start_sums(layer):
+        for unit in unit_order:
+            unit_stage(layer, unit, 0)
+
+    for step in range(early_tiles, tiles):
+        join1(step)
+    for step in range(early_tiles, tiles):
+        grad0[:, cols_at(step * TILE - halo, TILE)] += backward0(step)
+        if step == early_tiles:
+            on(c == 1, lambda: start_sums(1))
+    give(1, 2, grad1_low, grad_ref)
+    unit_out(0, [dres0[...], all_times(full)])
+    unit_conv(
+        0,
+        jnp.concatenate([xf[chunk] for chunk in range(chunks)], axis=1),
+        jnp.concatenate([xf[chunk + 1] for chunk in range(chunks)], axis=1),
+    )
+
+    arrive(past0_in, past0_at, has_next)
+
+    def join0(step, carry):
+        at = cols_at(step * TILE, TILE)
+        grad0_low[:, at] = grad0[:, at].astype(bf16)
+        return carry
+
+    lax.fori_loop(0, (span - halo) // TILE, join0, None)
+
+    def join0_late(step, carry):
+        at = cols_at(step * TILE + span - halo, TILE)
+        grad0_low[:, at] = (
+            grad0[:, at] + past0_in[:, cols_at(step * TILE, TILE)].astype(f32)
+        ).astype(bf16)
+        return carry
+
+    lax.fori_loop(0, halo // TILE, join0_late, None)
+    give(0, 2, grad0_low, grad_ref)
+
+    on(c == 0, lambda: in_order_of_arrival(0, 0, unit_order))
+    on(c == 1, lambda: in_order_of_arrival(1, 1, unit_order))
+    for unit in range(UNITS):
+        here = pl.ds(unit * unit_rows, unit_rows)
+        pltpu.make_async_copy(
+            final.at[here], weight_ref.at[here], local_sem.at[stored_at + unit]
+        ).wait()
+    pltpu.make_async_copy(
+        small_sum.at[1 + depth], small_ref, local_sem.at[stored_at + UNITS]
+    ).wait()
+    for kind, target in enumerate((res_ref, skipped_ref, grad_ref)):
+        arrive(target.at[oc], result_at[kind])
+    for copy, cond in locals_pending:
+        when(cond, copy.wait)
+    for wait, cond in pending:
+        when(cond, wait)
+    assert counts["send"] <= send_sem.shape[0], counts
+    assert counts["recv"] <= recv_sem.shape[0], counts
+    assert counts["local"] <= local_sem.shape[0], counts
+
+
+def run_layers(
+    x_in, skip_in, cot_res, cot_skip, lengths, speakers, conv_view, out_weight, table, n_seq
+):
+    micro, local, span = x_in.shape
+    full = out_weight.shape[1] // 2
+    gate_local = out_weight.shape[0]
+    gates = 2 * gate_local
+    bf16, f32 = jnp.bfloat16, jnp.float32
+    halo = FIRST_DILATION
+    rows = 3 * full
+    depth = (n_seq // 2).bit_length()
+    width = 2 * gate_local
+    any_spec = pl.BlockSpec(memory_space=pl.ANY)
+    scratch = [
+        (conv_view.shape, f32),
+        (out_weight.shape, f32),
+        (table.shape, f32),
+        ((span // halo + 1, full, halo), bf16),
+        ((2, 2, 2 * full + 16, width), bf16),
+        ((2, 2 * width, 2 * full), bf16),
+        ((2, gates, 2 * full), bf16),
+        ((2, 3 * local, gates), bf16),
+        ((2, 2 * width, 128), f32),
+        ((full, span), bf16),
+        ((full, 128), bf16),
+        ((full, 128), bf16),
+        ((full, span), bf16),
+        ((2, gates, span), f32),
+        ((2, gates, span), f32),
+        ((2, gates, span), bf16),
+        ((span // TILE, 2 * full, TILE), bf16),
+        ((full, span), bf16),
+        ((2, 2 * width, span), bf16),
+        ((full, span), f32),
+        ((full, span + 128), f32),
+        ((full, 128), bf16),
+        ((full, 128), bf16),
+        ((local, span), f32),
+        ((local, span), f32),
+        ((local, span), f32),
+        ((local, span), f32),
+        ((2, local, span), bf16),
+        ((local, span), bf16),
+        ((local, span), bf16),
+        ((local, span), f32),
+        ((local, halo), bf16),
+        ((local, halo), bf16),
+        ((local, span), bf16),
+        ((2, 2, 8, 128), f32),
+        ((2, rows, width), bf16),
+        ((rows, width), bf16),
+        ((rows, width), bf16),
+        ((rows, width), bf16),
+        ((2, 16, width), f32),
+        ((2 + depth, 16, width), f32),
+        ((2 + depth, 16, width), f32),
+    ]
+    result = jax.ShapeDtypeStruct((micro, local, span), bf16)
+    return pl.pallas_call(
+        functools.partial(layers_kernel, (full, local, gates, span, n_seq)),
+        out_shape=(
+            result,
+            result,
+            result,
+            jax.ShapeDtypeStruct((rows, width), bf16),
+            jax.ShapeDtypeStruct((16, width), f32),
+        ),
+        in_specs=[any_spec] * 4 + [pl.BlockSpec(memory_space=pltpu.SMEM)] * 2 + [any_spec] * 3,
+        out_specs=[any_spec] * 5,
+        scratch_shapes=[pltpu.VMEM(shape, kind) for shape, kind in scratch]
+        + [
+            pltpu.SemaphoreType.DMA((224,)),
+            pltpu.SemaphoreType.DMA((144,)),
+            pltpu.SemaphoreType.DMA((32,)),
+        ],
+        compiler_params=pltpu.CompilerParams(
+            collective_id=0, has_side_effects=True, vmem_limit_bytes=62 * 1024 * 1024
+        ),
+        cost_estimate=pl.CostEstimate(
+            flops=14_000_000_000, bytes_accessed=20_000_000, transcendentals=2_000_000
+        ),
+    )(x_in, skip_in, cot_res, cot_skip, lengths, speakers, conv_view, out_weight, table)
+
+
+def lane_view(value):
+    _, taps, full, halves, gate_local = value.shape
+    blocks = gate_local // 128
+    value = value.reshape(taps * full, halves, blocks, 128).transpose(0, 2, 1, 3)
+    return value.reshape(taps * full * halves * blocks, 128)
+
+
+def lane_back(value, shape):
+    _, taps, full, halves, gate_local = shape
+    blocks = gate_local // 128
+    value = value.reshape(taps * full, blocks, halves, 128).transpose(0, 2, 1, 3)
+    return value.reshape(shape)
+
+
+def update_kernel(
+    full,
+    lengths_ref,
+    speakers_ref,
+    small_ref,
+    conv_grad_in,
+    out_grad_in,
+    conv_w,
+    conv_m,
+    conv_v,
+    out_w,
+    out_m,
+    out_v,
+    table_w,
+    table_m,
+    table_v,
+    res_in,
+    skip_in,
+    grad_in,
+    res_out,
+    skip_out,
+    grad_out,
+    rms_out,
+    conv_g,
+    conv_w_new,
+    conv_m_new,
+    conv_v_new,
+    out_g,
+    out_w_new,
+    out_m_new,
+    out_v_new,
+    table_g,
+    table_w_new,
+    table_m_new,
+    table_v_new,
+):
+    f32 = jnp.float32
+
+    def update(gradient, weight, moment, second, rate, targets):
+        new = adamw(weight[...], moment[...], second[...], gradient, rate)
+        for target, value in zip(targets, new):
+            target[...] = value
+
+    for source, target in ((res_in, res_out), (skip_in, skip_out), (grad_in, grad_out)):
+        target[...] = source[...].astype(f32)
+
+    taps, width = conv_grad_in.shape
+    blocks = width // 128
+    for block in range(blocks):
+        half, lane = block // (blocks // 2), block % (blocks // 2)
+        conv_g[pl.ds(lane * 2 + half, taps, stride=blocks), :] = conv_grad_in[
+            :, block * 128 : (block + 1) * 128
+        ].astype(f32)
+    update(conv_g[...], conv_w, conv_m, conv_v, 0.03, (conv_w_new, conv_m_new, conv_v_new))
+
+    out_g[...] = out_grad_in[...].astype(f32).T
+    update(out_g[...], out_w, out_m, out_v, 0.1, (out_w_new, out_m_new, out_v_new))
+
+    half = width // 2
+    row = lax.broadcasted_iota(jnp.int32, table_w.shape, 0) + pl.program_id(0) * table_w.shape[0]
+    total = jnp.zeros(table_w.shape, f32)
+    for micro in range(2):
+        sums = jnp.concatenate(
+            [small_ref[micro : micro + 1, 0:half], small_ref[micro : micro + 1, half:]], axis=0
+        )
+        total = total + jnp.where(row == speakers_ref[micro], sums[None], 0.0)
+    table_g[...] = total
+    update(total, table_w, table_m, table_v, 0.3, (table_w_new, table_m_new, table_v_new))
+
+    @pl.when(pl.program_id(0) == 0)
+    def _():
+        counted = (lengths_ref[0] + lengths_ref[1]).astype(f32) * full
+        squares = [
+            jnp.sum(small_ref[8:16, part * 128 : (part + 1) * 128], axis=(0, 1), keepdims=True)
+            for part in range(2)
+        ]
+        at = lax.broadcasted_iota(jnp.int32, (1, 2), 1)
+        rms_out[...] = jnp.sqrt(jnp.where(at == 0, squares[0], squares[1]) / counted)
+
+
+def run_update(lengths, speakers, small, weights, conv_parts, out_parts, table_parts, results):
+    steps = 8
+    width = weights.shape[1]
+    gate_local, full = out_parts[0].shape[0], out_parts[0].shape[1] // 2
+    f32 = jnp.float32
+
+    def rows(value, axis=0):
+        shape = list(value.shape)
+        shape[axis] = pl.cdiv(shape[axis], steps)
+        return pl.BlockSpec(tuple(shape), lambda i: tuple(i if at == axis else 0 for at in range(len(shape))))
+
+    def whole(shape):
+        return pl.BlockSpec(tuple(shape), lambda i: (0,) * len(shape))
+
+    conv_block, out_block = 2 * full // steps, 2 * full // steps
+    out_first = 2 * full // out_block
+    smem = pl.BlockSpec(memory_space=pltpu.SMEM)
+    like = [jax.ShapeDtypeStruct(value.shape, f32) for value in (results[0], conv_parts[0], out_parts[0], table_parts[0])]
+    specs = [rows(results[0], 1), rows(conv_parts[0]), rows(out_parts[0], 1), rows(table_parts[0])]
+    return pl.pallas_call(
+        functools.partial(update_kernel, full),
+        grid=(steps,),
+        out_shape=(
+            *[like[0]] * 3,
+            jax.ShapeDtypeStruct((1, 2), f32),
+            *[like[1]] * 4,
+            *[like[2]] * 4,
+            *[like[3]] * 4,
+        ),
+        in_specs=[
+            smem,
+            smem,
+            whole(small.shape),
+            pl.BlockSpec((conv_block, width), lambda i: (i, 0)),
+            pl.BlockSpec(
+                (out_block, gate_local),
+                lambda i: (out_first + i % (steps // 2), i // (steps // 2)),
+            ),
+            *[specs[1]] * 3,
+            *[specs[2]] * 3,
+            *[specs[3]] * 3,
+            *[specs[0]] * 3,
+        ],
+        out_specs=(
+            *[specs[0]] * 3,
+            whole((1, 2)),
+            *[specs[1]] * 4,
+            *[specs[2]] * 4,
+            *[specs[3]] * 4,
+        ),
+        compiler_params=pltpu.CompilerParams(
+            dimension_semantics=("arbitrary",), vmem_limit_bytes=62 * 1024 * 1024
+        ),
+        cost_estimate=pl.CostEstimate(
+            flops=20_000_000, bytes_accessed=32_000_000, transcendentals=1_000_000
+        ),
+    )(
+        lengths,
+        speakers,
+        small,
+        weights,
+        weights,
+        *conv_parts,
+        *out_parts,
+        *table_parts,
+        *results,
+    )
+
+
+def fast_shards(
+    n_seq,
+    x_in,
+    skip_in,
+    cot_res,
+    cot_skip,
+    lengths,
+    speakers,
+    conv_weight,
+    conv_m,
+    conv_v,
+    out_weight,
+    out_m,
+    out_v,
+    speaker_table,
+    table_m,
+    table_v,
+):
+    views = [lane_view(value) for value in (conv_weight, conv_m, conv_v)]
+    res, skipped, grads, weights, small = run_layers(
+        x_in,
+        skip_in,
+        cot_res,
+        cot_skip,
+        lengths,
+        speakers,
+        views[0],
+        out_weight[0],
+        speaker_table[0],
+        n_seq,
+    )
+    results = run_update(
+        lengths,
+        speakers,
+        small,
+        weights,
+        views,
+        [out_weight[0], out_m[0], out_v[0]],
+        [speaker_table[0], table_m[0], table_v[0]],
+        [res, skipped, grads],
+    )
+    wide, rms_out = results[0:3], results[3]
+    conv_parts = [lane_back(value, conv_weight.shape) for value in results[4:8]]
+    return (
+        *[value[None] for value in wide],
+        rms_out,
+        *conv_parts,
+        *[value[None] for value in results[8:12]],
+        *[value[None] for value in results[12:16]],
+    )
 
 
 def shards(
@@ -283,4 +1380,12 @@
         P("section", None, None, "mp"),
         P("section", None, None, "mp"),
     )
-    return jax.shard_map(shards, mesh=mesh, in_specs=in_specs, out_specs=out_specs, check_vma=False)
+    n_seq = mesh.shape["seq"]
+    fits = mesh.shape["mp"] == 2 and n_seq in (4, 8, 16)
+    return jax.shard_map(
+        functools.partial(fast_shards, n_seq) if fits else shards,
+        mesh=mesh,
+        in_specs=in_specs,
+        out_specs=out_specs,
+        check_vma=False,
+    )

time: 883 us -> 140 us (0.16)
  waiting for transfers between devices: 591 us -> 0 us
  Pallas kernels: 0 us -> 138 us
  other arithmetic: 75.2 us -> 0 us
  matrix products: 59.9 us -> 0 us
  local copies, waits for them, and re-layouts: 50.7 us -> 0 us
  blocking collectives: 43.7 us -> 0 us
  starting transfers between devices: 29.3 us -> 0 us
  between operations: 23.9 us -> 0.83 us
    reduce_scatter x6 -> x0, waiting for transfers between devices: 276 us -> none  [the longest x3 150 us: shards(): lax.psum_scatter(tap_terms.reshape(2, full_res, block_length_rows), 'mp',...]
    all_gather x6 -> x0, waiting for transfers between devices: 170 us -> none  [the longest x3 92.5 us: shards(): lax.all_gather(tap_rows, 'mp', axis=1, tiled=True)]
    pallas_call x0 -> x2, Pallas kernels: none -> 138 us  [the longest x1 122 us: run_layers(): pl.pallas_call(functools.partial(layers_kernel, (full, local, gates, span...]
    psum x1 -> x0, waiting for transfers between devices: 79.7 us -> none  [shards(): lax.psum((conv_acc, out_acc, table_acc), 'seq')]
    ppermute x12 -> x0, waiting for transfers between devices: 64.9 us -> none  [passed_along(): lax.ppermute(value, axis, [(source, source + steps) for source in range(f...]
    dot_general x21 -> x0, matrix products: 59.9 us -> none  [the longest x3 13.5 us: shards(): lax.dot_general(conv_matrix, forward_tap_full, contract_first, preferred_...]
    psum x1 -> x0, blocking collectives: 43.7 us -> none  [shards(): lax.psum((square_res, square_branch, counted), ('seq', 'mp'))]
    ppermute x12 -> x0, starting transfers between devices: 28.4 us -> none  [passed_along(): lax.ppermute(value, axis, [(source, source + steps) for source in range(f...]
  transfers between devices with their start and end apart: 25 -> 0, of which waited for: 24 -> 0; matrix products, arithmetic and copies ran while one was open for 11% -> 0% of each run, Pallas kernels for 0% -> 0%
where the time goes in v1:
time: 140 us; the launch traced here: 139 us
  Pallas kernels  138 us (99%)
    pallas_call x1, Pallas kernels, run_layers(): pl.pallas_call(functools.partial(layers_kernel, (full, local, gates, span...  122 us
    pallas_call x1, Pallas kernels, run_update(): pl.pallas_call(functools.partial(update_kernel, full), grid=(steps,), out...  16.5 us

profile of v1, /device:TPU:0, one launch (start us, length us, event | category | flops | bytes accessed | tf_op | source)
XLA Modules:
  0.0 139.3 jit_solution(10610262099869752126)
XLA Ops:
  0.6 121.9 %shard_map.270 = (bf16[2,256,1024]{2,1,0:T(8,128)(2,1)}, bf16[2,256,1024]{2,1,0:T(8,128)(2,1)}, bf16[2,256,1024]{2,1,0:T(8,128)(2,1)}, bf16[1536,512]{1,0:T(8,128)(2,1)}, f32[16,512]{1,0:T(8,128)}) custom-call(bf16[2,256,1024]{2,1,0:T(8,128)(2,1)} %x_ref.1, f32[2,256,1024]{2,1,0:T(8,128)} %skip_ref.1, f32[2,256,1024]{2,1,0:T(8,128)} %cot_res_ref.1, ...), custom_call_target="tpu_custom_call" | custom-call | flops 14000000000 | bytes 20000000 | tf_op jit(solution)/shard_map/pallas_call | solution.py:891
  122.6 16.5 %shard_map.271 = (f32[2,256,1024]{2,1,0:T(8,128)}, f32[2,256,1024]{2,1,0:T(8,128)}, f32[2,256,1024]{2,1,0:T(8,128)}, f32[1,2]{1,0:T(1,128)}, f32[4096,128]{1,0:T...) custom-call(s32[2]{0:T(128)} %lengths_ref.3, ...), custom_call_target="tpu_custom_call" | custom-call | flops 20000000 | bytes 32000000 | tf_op jit(solution)/shard_map/pallas_call | solution.py:1030

commit v2 on v1

--- a/solution.py
+++ b/solution.py
@@ -12,8 +12,8 @@
 STEP = 10
 MESH = pl.DeviceIdType.MESH
 TILE = 256
-UNITS = 6
-Z_FIRST = 3
+UNITS = 3
+Z_FIRST = 1
 
 beta_one = 0.9
 beta_two = 0.999
@@ -760,7 +760,7 @@
         for stage in range(small_next, 2 + depth):
             small_stage(layer, stage)
 
-    unit_order = [4, 5, 0, 1, 2, 3]
+    unit_order = [2, 0, 1]
 
     def all_times(first):
         rows = slice(first, first + full)
@@ -809,7 +809,11 @@
     lax.fori_loop(0, halo // TILE, join0_late, None)
     give(0, 2, grad0_low, grad_ref)
 
-    on(c == 0, lambda: in_order_of_arrival(0, 0, unit_order))
+    on(c == 0, lambda: start_sums(0))
+    for wait, cond in pending:
+        when(cond, wait)
+    pending.clear()
+    on(c == 0, lambda: in_order_of_arrival(0, 1, unit_order))
     on(c == 1, lambda: in_order_of_arrival(1, 1, unit_order))
     for unit in range(UNITS):
         here = pl.ds(unit * unit_rows, unit_rows)

time: 140 us -> 139 us (level)
  no operation moved by 1% of the time
where the time goes in v2:
time: 139 us; the launch traced here: 138 us
  Pallas kernels  138 us (99%)
    pallas_call x1, Pallas kernels, run_layers(): pl.pallas_call(functools.partial(layers_kernel, (full, local, gates, span...  121 us
    pallas_call x1, Pallas kernels, run_update(): pl.pallas_call(functools.partial(update_kernel, full), grid=(steps,), out...  16.5 us

profile of v2, /device:TPU:0, one launch (start us, length us, event | category | flops | bytes accessed | tf_op | source)
XLA Modules:
  0.0 138.4 jit_solution(17218415252076167628)
XLA Ops:
  0.6 121.1 %shard_map.270 = (bf16[2,256,1024]{2,1,0:T(8,128)(2,1)}, bf16[2,256,1024]{2,1,0:T(8,128)(2,1)}, bf16[2,256,1024]{2,1,0:T(8,128)(2,1)}, bf16[1536,512]{1,0:T(8,128)(2,1)}, f32[16,512]{1,0:T(8,128)}) custom-call(bf16[2,256,1024]{2,1,0:T(8,128)(2,1)} %x_ref.1, f32[2,256,1024]{2,1,0:T(8,128)} %skip_ref.1, f32[2,256,1024]{2,1,0:T(8,128)} %cot_res_ref.1, ...), custom_call_target="tpu_custom_call" | custom-call | flops 14000000000 | bytes 20000000 | tf_op jit(solution)/shard_map/pallas_call | solution.py:895
  121.7 16.5 %shard_map.271 = (f32[2,256,1024]{2,1,0:T(8,128)}, f32[2,256,1024]{2,1,0:T(8,128)}, f32[2,256,1024]{2,1,0:T(8,128)}, f32[1,2]{1,0:T(1,128)}, f32[4096,128]{1,0:T...) custom-call(s32[2]{0:T(128)} %lengths_ref.3, ...), custom_call_target="tpu_custom_call" | custom-call | flops 20000000 | bytes 32000000 | tf_op jit(solution)/shard_map/pallas_call | solution.py:1034

commit v3 on v2

--- a/solution.py
+++ b/solution.py
@@ -11,9 +11,9 @@
 FIRST_DILATION = 512
 STEP = 10
 MESH = pl.DeviceIdType.MESH
-TILE = 256
-UNITS = 3
-Z_FIRST = 1
+TILE = 512
+UNITS = 6
+Z_FIRST = 3
 
 beta_one = 0.9
 beta_two = 0.999
@@ -602,16 +602,10 @@
     for step in range(tiles):
         for part in range(2):
             arrive(cot_piece(step, part, ox), cot_at + step * 2 + part)
-        tile = step - (tiles - early_tiles)
-        if tile >= 0:
-            join1(tile)
         backward1(step)
-        if tile >= 0:
-            past0_out[:, cols_at(tile * TILE, TILE)] = backward0(tile).astype(bf16)
         if step == 0:
             edge_out[...] = past_grad1[:, 0:128].astype(bf16)
             send(lambda: edge_out, lambda: edge_in, prev_dev, lambda: edge_at, has_prev)
-    send(lambda: past0_out, lambda: past0_in, prev_dev, lambda: past0_at, has_prev)
 
     total_rows = 3 * full
     unit_rows = total_rows // UNITS
@@ -653,10 +647,10 @@
 
     def unit_out(layer, parts):
         hidden = hid[layer, rows_at(x * gate_local, gate_local), :]
-        product = dot_last(jnp.concatenate(parts, axis=0), hidden)
-        for part in range(2):
-            acc[layer, pl.ds(2 * full, full), pl.ds(part * gate_local, gate_local)] = product[
-                part * full : (part + 1) * full
+        product = dot_last(hidden, jnp.concatenate(parts, axis=0))
+        for part in range(2 * full // width):
+            acc[layer, pl.ds(2 * full + part * gate_local, gate_local), :] = product[
+                :, part * width : (part + 1) * width
             ].astype(bf16)
         to_core(layer, 2 * full, full)
 
@@ -760,7 +754,7 @@
         for stage in range(small_next, 2 + depth):
             small_stage(layer, stage)
 
-    unit_order = [2, 0, 1]
+    unit_order = [4, 5, 0, 1, 2, 3]
 
     def all_times(first):
         rows = slice(first, first + full)
@@ -776,12 +770,14 @@
         for unit in unit_order:
             unit_stage(layer, unit, 0)
 
-    for step in range(early_tiles, tiles):
+    for step in range(tiles):
         join1(step)
+    for step in range(early_tiles):
+        past0_out[:, cols_at(step * TILE, TILE)] = backward0(step).astype(bf16)
+    send(lambda: past0_out, lambda: past0_in, prev_dev, lambda: past0_at, has_prev)
+    on(c == 1, lambda: start_sums(1))
     for step in range(early_tiles, tiles):
         grad0[:, cols_at(step * TILE - halo, TILE)] += backward0(step)
-        if step == early_tiles:
-            on(c == 1, lambda: start_sums(1))
     give(1, 2, grad1_low, grad_ref)
     unit_out(0, [dres0[...], all_times(full)])
     unit_conv(
@@ -938,7 +934,8 @@
     speakers_ref,
     small_ref,
     conv_grad_in,
-    out_grad_in,
+    out_left,
+    out_right,
     conv_w,
     conv_m,
     conv_v,
@@ -987,7 +984,8 @@
         ].astype(f32)
     update(conv_g[...], conv_w, conv_m, conv_v, 0.03, (conv_w_new, conv_m_new, conv_v_new))
 
-    out_g[...] = out_grad_in[...].astype(f32).T
+    out_g[:, 0:width] = out_left[...].astype(f32)
+    out_g[:, width:] = out_right[...].astype(f32)
     update(out_g[...], out_w, out_m, out_v, 0.1, (out_w_new, out_m_new, out_v_new))
 
     half = width // 2
@@ -1026,11 +1024,11 @@
     def whole(shape):
         return pl.BlockSpec(tuple(shape), lambda i: (0,) * len(shape))
 
-    conv_block, out_block = 2 * full // steps, 2 * full // steps
-    out_first = 2 * full // out_block
+    conv_block, out_block = 2 * full // steps, gate_local // steps
+    left, right = 2 * full // out_block, (2 * full + gate_local) // out_block
     smem = pl.BlockSpec(memory_space=pltpu.SMEM)
     like = [jax.ShapeDtypeStruct(value.shape, f32) for value in (results[0], conv_parts[0], out_parts[0], table_parts[0])]
-    specs = [rows(results[0], 1), rows(conv_parts[0]), rows(out_parts[0], 1), rows(table_parts[0])]
+    specs = [rows(results[0], 1), rows(conv_parts[0]), rows(out_parts[0]), rows(table_parts[0])]
     return pl.pallas_call(
         functools.partial(update_kernel, full),
         grid=(steps,),
@@ -1046,10 +1044,8 @@
             smem,
             whole(small.shape),
             pl.BlockSpec((conv_block, width), lambda i: (i, 0)),
-            pl.BlockSpec(
-                (out_block, gate_local),
-                lambda i: (out_first + i % (steps // 2), i // (steps // 2)),
-            ),
+            pl.BlockSpec((out_block, width), lambda i: (left + i, 0)),
+            pl.BlockSpec((out_block, width), lambda i: (right + i, 0)),
             *[specs[1]] * 3,
             *[specs[2]] * 3,
             *[specs[3]] * 3,
@@ -1072,6 +1068,7 @@
         lengths,
         speakers,
         small,
+        weights,
         weights,
         weights,
         *conv_parts,

time: 139 us -> 143 us (1.029)
  Pallas kernels: 138 us -> 142 us
    pallas_call x1, Pallas kernels: 121 us -> 126 us  [run_layers(): pl.pallas_call(functools.partial(layers_kernel, (full, local, gates, span...]
where the time goes in v3:
time: 143 us
  Pallas kernels  142 us (99%)
    pallas_call x1, Pallas kernels, run_layers(): pl.pallas_call(functools.partial(layers_kernel, (full, local, gates, span...  126 us
    pallas_call x1, Pallas kernels, run_update(): pl.pallas_call(functools.partial(update_kernel, full), grid=(steps,), out...  15.7 us

profile of v3, /device:TPU:0, one launch (start us, length us, event | category | flops | bytes accessed | tf_op | source)
XLA Modules:
  0.0 142.9 jit_solution(2678090377973380606)
XLA Ops:
  0.6 126.4 %shard_map.270 = (bf16[2,256,1024]{2,1,0:T(8,128)(2,1)}, bf16[2,256,1024]{2,1,0:T(8,128)(2,1)}, bf16[2,256,1024]{2,1,0:T(8,128)(2,1)}, bf16[1536,512]{1,0:T(8,128)(2,1)}, f32[16,512]{1,0:T(8,128)}) custom-call(bf16[2,256,1024]{2,1,0:T(8,128)(2,1)} %x_ref.1, f32[2,256,1024]{2,1,0:T(8,128)} %skip_ref.1, f32[2,256,1024]{2,1,0:T(8,128)} %cot_res_ref.1, ...), custom_call_target="tpu_custom_call" | custom-call | flops 14000000000 | bytes 20000000 | tf_op jit(solution)/shard_map/pallas_call | solution.py:891
  127.1 15.7 %shard_map.271 = (f32[2,256,1024]{2,1,0:T(8,128)}, f32[2,256,1024]{2,1,0:T(8,128)}, f32[2,256,1024]{2,1,0:T(8,128)}, f32[1,2]{1,0:T(1,128)}, f32[4096,128]{1,0:T...) custom-call(s32[2]{0:T(128)} %lengths_ref.3, ...), custom_call_target="tpu_custom_call" | custom-call | flops 20000000 | bytes 32000000 | tf_op jit(solution)/shard_map/pallas_call | solution.py:1032

commit v4 on v2

--- a/solution.py
+++ b/solution.py
@@ -221,16 +221,13 @@
 
     own_rows, other_rows = rows_at(x * local, local), rows_at(ox * local, local)
     got_conv = fetch(conv_ref, conv_wide)
-    got_table = fetch(table_ref, table_wide)
-    got_out = fetch(out_ref, out_wide)
-    got_cot_a = fetch(cot_res_ref.at[c], cot_a)
-    got_cot_b = fetch(cot_skip_ref.at[c], cot_b)
     chunks = span // halo
     got_x = [
         fetch(x_ref.at[c, :, pl.ds(chunk * halo, halo)], xf.at[chunk + 1, own_rows])
-        for chunk in range(chunks)
+        for chunk in reversed(range(chunks))
     ]
-    got_skip = fetch(skip_ref.at[c], skip_sum)
+    got_table = fetch(table_ref, table_wide)
+    got_out = fetch(out_ref, out_wide)
 
     def cast_conv(step, carry):
         for block in range(width // 128):
@@ -242,6 +239,9 @@
         return carry
 
     got_conv.wait()
+    got_cot_a = fetch(cot_res_ref.at[c], cot_a)
+    got_cot_b = fetch(cot_skip_ref.at[c], cot_b)
+    got_skip = fetch(skip_ref.at[c], skip_sum)
     lax.fori_loop(0, 2 * full // 256, cast_conv, None)
     got_table.wait()
     marks = lax.broadcasted_iota(jnp.int32, (16, width), 0)
@@ -440,6 +440,7 @@
         turn_all(0, x)
 
     on(c == 0, spread_out)
+    turn_all(1, x)
     on(c == 0, spread_last)
 
     on(c == 1, all_from_core)
@@ -521,7 +522,6 @@
     give(0, 0, in1.at[own_rows], res_ref)
     give(0, 1, skip_low.at[0], skipped_ref)
 
-    turn_all(1, x)
     on(c == 0, all_from_core)
     turn_all(1, ox)
 

time: 139 us -> 139 us (level)
  no operation moved by 1% of the time
where the time goes in v4:
time: 139 us; the launch traced here: 138 us
  Pallas kernels  138 us (99%)
    pallas_call x1, Pallas kernels, run_layers(): pl.pallas_call(functools.partial(layers_kernel, (full, local, gates, span...  121 us
    pallas_call x1, Pallas kernels, run_update(): pl.pallas_call(functools.partial(update_kernel, full), grid=(steps,), out...  16.5 us

profile of v4, /device:TPU:0, one launch (start us, length us, event | category | flops | bytes accessed | tf_op | source)
XLA Modules:
  0.0 138.4 jit_solution(15522524263682403954)
XLA Ops:
  0.6 121.1 %shard_map.270 = (bf16[2,256,1024]{2,1,0:T(8,128)(2,1)}, bf16[2,256,1024]{2,1,0:T(8,128)(2,1)}, bf16[2,256,1024]{2,1,0:T(8,128)(2,1)}, bf16[1536,512]{1,0:T(8,128)(2,1)}, f32[16,512]{1,0:T(8,128)}) custom-call(bf16[2,256,1024]{2,1,0:T(8,128)(2,1)} %x_ref.1, f32[2,256,1024]{2,1,0:T(8,128)} %skip_ref.1, f32[2,256,1024]{2,1,0:T(8,128)} %cot_res_ref.1, ...), custom_call_target="tpu_custom_call" | custom-call | flops 14000000000 | bytes 20000000 | tf_op jit(solution)/shard_map/pallas_call | solution.py:895
  121.7 16.5 %shard_map.271 = (f32[2,256,1024]{2,1,0:T(8,128)}, f32[2,256,1024]{2,1,0:T(8,128)}, f32[2,256,1024]{2,1,0:T(8,128)}, f32[1,2]{1,0:T(1,128)}, f32[4096,128]{1,0:T...) custom-call(s32[2]{0:T(128)} %lengths_ref.3, ...), custom_call_target="tpu_custom_call" | custom-call | flops 20000000 | bytes 32000000 | tf_op jit(solution)/shard_map/pallas_call | solution.py:1034

commit v5 on v4

--- a/solution.py
+++ b/solution.py
@@ -632,17 +632,23 @@
                 c != layer,
             )
 
-    def unit_conv(layer, past, now):
-        taps = jnp.concatenate([past, now, jnp.ones((16, span), bf16)], axis=0)
-        product = dot_last(taps, dpre[layer, rows_at(x * width, width), :])
-        acc[layer, 0 : 2 * full, :] = product[0 : 2 * full].astype(bf16)
-        sums = product[2 * full : 2 * full + 8]
+    def unit_conv(layer, past, now, between=None):
+        def part(first, taps):
+            product = dot_last(taps, dpre[layer, rows_at(x * width, width), :])
+            acc[layer, pl.ds(first, full), :] = product[0:full].astype(bf16)
+            to_core(layer, first, full)
+            return product
+
+        part(0, past)
+        if between is not None:
+            between()
+        product = part(full, jnp.concatenate([now, jnp.ones((16, span), bf16)], axis=0))
+        sums = product[full : full + 8]
         mark = lax.broadcasted_iota(jnp.int32, sums.shape, 0)
         small[layer, 0:8, :] = jnp.where(mark == c, sums, 0.0)
         small[layer, 8:16, :] = jnp.zeros((8, width), f32)
         small[layer, 8:16, 0:128] = stats[layer, 0]
         small[layer, 8:16, 128:256] = stats[layer, 1]
-        to_core(layer, 0, 2 * full)
         send(
             lambda: small.at[layer],
             lambda: small_in.at[0],
@@ -772,8 +778,8 @@
     arrive(edge_in, edge_at, has_next)
     past_grad1[:, span : span + 128] = edge_in[...].astype(f32)
 
-    def start_sums(layer):
-        for unit in unit_order:
+    def start_sums(layer, units):
+        for unit in units:
             unit_stage(layer, unit, 0)
 
     for step in range(early_tiles, tiles):
@@ -781,13 +787,14 @@
     for step in range(early_tiles, tiles):
         grad0[:, cols_at(step * TILE - halo, TILE)] += backward0(step)
         if step == early_tiles:
-            on(c == 1, lambda: start_sums(1))
+            on(c == 1, lambda: start_sums(1, unit_order))
     give(1, 2, grad1_low, grad_ref)
     unit_out(0, [dres0[...], all_times(full)])
     unit_conv(
         0,
         jnp.concatenate([xf[chunk] for chunk in range(chunks)], axis=1),
         jnp.concatenate([xf[chunk + 1] for chunk in range(chunks)], axis=1),
+        lambda: on(c == 0, lambda: start_sums(0, unit_order[:1])),
     )
 
     arrive(past0_in, past0_at, has_next)
@@ -809,7 +816,7 @@
     lax.fori_loop(0, halo // TILE, join0_late, None)
     give(0, 2, grad0_low, grad_ref)
 
-    on(c == 0, lambda: start_sums(0))
+    on(c == 0, lambda: start_sums(0, unit_order[1:]))
     for wait, cond in pending:
         when(cond, wait)
     pending.clear()

time: 139 us -> 139 us (level)
  no operation moved by 1% of the time
where the time goes in v5:
time: 139 us
  Pallas kernels  138 us (99%)
    pallas_call x1, Pallas kernels, run_layers(): pl.pallas_call(functools.partial(layers_kernel, (full, local, gates, span...  121 us
    pallas_call x1, Pallas kernels, run_update(): pl.pallas_call(functools.partial(update_kernel, full), grid=(steps,), out...  16.5 us

profile of v5, /device:TPU:0, one launch (start us, length us, event | category | flops | bytes accessed | tf_op | source)
XLA Modules:
  0.0 138.6 jit_solution(14644719299599602938)
XLA Ops:
  0.6 121.3 %shard_map.270 = (bf16[2,256,1024]{2,1,0:T(8,128)(2,1)}, bf16[2,256,1024]{2,1,0:T(8,128)(2,1)}, bf16[2,256,1024]{2,1,0:T(8,128)(2,1)}, bf16[1536,512]{1,0:T(8,128)(2,1)}, f32[16,512]{1,0:T(8,128)}) custom-call(bf16[2,256,1024]{2,1,0:T(8,128)(2,1)} %x_ref.1, f32[2,256,1024]{2,1,0:T(8,128)} %skip_ref.1, f32[2,256,1024]{2,1,0:T(8,128)} %cot_res_ref.1, ...), custom_call_target="tpu_custom_call" | custom-call | flops 14000000000 | bytes 20000000 | tf_op jit(solution)/shard_map/pallas_call | solution.py:902
  121.9 16.5 %shard_map.271 = (f32[2,256,1024]{2,1,0:T(8,128)}, f32[2,256,1024]{2,1,0:T(8,128)}, f32[2,256,1024]{2,1,0:T(8,128)}, f32[1,2]{1,0:T(1,128)}, f32[4096,128]{1,0:T...) custom-call(s32[2]{0:T(128)} %lengths_ref.3, ...), custom_call_target="tpu_custom_call" | custom-call | flops 20000000 | bytes 32000000 | tf_op jit(solution)/shard_map/pallas_call | solution.py:1041
